TPU v7x, 128 devices: a whole 4x4x4 slice. The times are simulated.
128 devices in a mesh: seq: 8 (over y_lo, x), head: 16 (over z, y_hi, core).
Axes of the slice: x: 4, y: 4 (y_hi: 2, y_lo: 2; y = y_hi * 2 + y_lo), z: 4, core: 2. Of those that a mesh axis runs over, the one named last changes fastest.
Arguments:
- block_in: bfloat16 [16384, 2048], P('seq', 'head'), may hold values from -6 to 6
- cotangent: bfloat16 [16384, 2048], P('seq', 'head'), may hold values from -6 to 6
- norm_one: float32 [2048], P('head'), may hold values from 0.1 to 1.9
- rec_in: bfloat16 [2048, 2560], P('seq', 'head'), may hold values from -0.125 to 0.125
- rec_gate: bfloat16 [2048, 2560], P('seq', 'head'), may hold values from -0.125 to 0.125
- conv_weight: float32 [4, 2560], P(None, 'head'), may hold values from -3 to 3
- conv_bias: float32 [2560], P('head'), may hold values from -2 to 2
- rate_weight: float32 [16, 160, 160], P('head'), may hold values from -0.5 to 0.5
- rate_bias: float32 [2560], P('head'), may hold values from -3 to 3
- input_weight: float32 [16, 160, 160], P('head'), may hold values from -0.5 to 0.5
- input_bias: float32 [2560], P('head'), may hold values from -3 to 3
- decay_code: int32 [2560], P('head'), may hold values from 920 to 3071, as said below
- rec_out: bfloat16 [2560, 2048], P('head', 'seq'), may hold values from -0.125 to 0.125
- norm_two: float32 [2048], P('head'), may hold values from 0.1 to 1.9
- mlp_gate: bfloat16 [2048, 6144], P('seq', 'head'), may hold values from -0.125 to 0.125
- mlp_up: bfloat16 [2048, 6144], P('seq', 'head'), may hold values from -0.125 to 0.125
- mlp_down: bfloat16 [6144, 2048], P('head', 'seq'), may hold values from -0.15625 to 0.15625
Outputs:
- block_out: bfloat16 [16384, 2048], P('seq', 'head')
- grad_block_in: float32 [16384, 2048], P('seq', 'head')
- grad_norm_one: float32 [2048], P('head')
- grad_rec_in: float32 [2048, 2560], P('seq', 'head')
- grad_rec_gate: float32 [2048, 2560], P('seq', 'head')
- grad_conv_weight: float32 [4, 2560], P(None, 'head')
- grad_conv_bias: float32 [2560], P('head')
- grad_rate_weight: float32 [16, 160, 160], P('head')
- grad_rate_bias: float32 [2560], P('head')
- grad_input_weight: float32 [16, 160, 160], P('head')
- grad_input_bias: float32 [2560], P('head')
- grad_decay_param: float32 [2560], P('head')
- grad_rec_out: float32 [2560, 2048], P('head', 'seq')
- grad_norm_two: float32 [2048], P('head')
- grad_mlp_gate: float32 [2048, 6144], P('seq', 'head')
- grad_mlp_up: float32 [2048, 6144], P('seq', 'head')
- grad_mlp_down: float32 [6144, 2048], P('head', 'seq')
Inputs may be any that keep to these rules, and one draw needn't show every extreme that they name: `decay_code`: lambda = code / 256 for each channel.
All inputs are finite; a program needn't handle non-finite values.
Results may differ from a plain program's by a relative error of at most 0.015.
Values may be sent and summed in bfloat16 or wider, within the bound.
A program may use at most 256 MiB of HBM per device.

v0:
```python
import jax
import jax.numpy as jnp
from jax import lax
from jax.sharding import PartitionSpec as P

D = 2048
CONV = 4


HIGH = lax.Precision.HIGHEST
EPS = 1e-06


def from_behind(array, axis, by):
    size = lax.axis_size(axis)
    pairs = [(i, i + by) for i in range(size) if 0 <= i + by < size]
    return lax.ppermute(array, axis, pairs)


def prefix(part, axis, combine, identity, reverse):
    count = lax.axis_size(axis)
    place = lax.axis_index(axis)
    ahead = count - 1 - place if reverse else place
    gathered = jax.tree.map(lambda a: lax.all_gather(a, axis), part)
    state = jax.tree.map(lambda a, e: jnp.zeros_like(a) + jnp.asarray(e, a.dtype), part, identity)

    def one(turn, state):
        source = count - 1 - turn if reverse else turn
        return combine(
            state, jax.tree.map(lambda a: lax.dynamic_index_in_dim(a, source, 0, False), gathered)
        )

    return lax.fori_loop(0, ahead, one, state)


def pair_combine(earlier, later):
    return (earlier[0] * later[0], later[0] * earlier[1] + later[1])


def exact_gelu(values):
    return jax.nn.gelu(values, approximate=False)


def dot_plain(left_side, right_side):
    return jnp.dot(left_side, right_side, preferred_element_type=jnp.float32)


def dot_left_t(left_side, right_side):
    return lax.dot_general(
        left_side, right_side, (((0,), (0,)), ((), ())), preferred_element_type=jnp.float32
    )


def dot_right_t(left_side, right_side):
    return lax.dot_general(
        left_side, right_side, (((1,), (1,)), ((), ())), preferred_element_type=jnp.float32
    )


def norm_forward(values, gain_vec):
    summed = lax.psum(jnp.sum(values * values, axis=1), "head")
    inv_rms = lax.rsqrt(summed / D + EPS)
    return (values * inv_rms[:, None] * gain_vec[None, :], inv_rms)


def norm_backward(values, gain_vec, inv_rms, grad_normed):
    weighted = grad_normed * gain_vec[None, :]
    summed = lax.psum(jnp.sum(values * weighted, axis=1), "head")
    grad_values = (
        weighted * inv_rms[:, None] - values * (inv_rms * inv_rms * inv_rms * summed / D)[:, None]
    )
    grad_gain = jnp.sum(grad_normed * values * inv_rms[:, None], axis=0)
    return (grad_values, grad_gain)


def rows_gather(normed):
    return lax.all_gather(normed.astype(jnp.bfloat16), "head", axis=1, tiled=True)


def branch_sum(partial_rows):
    return lax.psum_scatter(partial_rows, "head", scatter_dimension=1, tiled=True)


def grads_gather(grad_rows):
    return lax.all_gather(grad_rows.astype(jnp.bfloat16), "head", axis=1, tiled=True)


def feature_sum(partial_rows):
    return lax.psum_scatter(partial_rows, "head", scatter_dimension=1, tiled=True)


def gate_piece(conv_out, rate_weight, rate_bias, input_weight, input_bias, decay_param):
    row_count = conv_out.shape[0]
    heads_local = rate_weight.shape[0]
    head_width = rate_weight.shape[1]
    split_in = conv_out.reshape(row_count, heads_local, head_width)
    rate_gate = jax.nn.sigmoid(
        jnp.einsum("lhi,hij->lhj", split_in, rate_weight, precision=HIGH).reshape(
            row_count, heads_local * head_width
        )
        + rate_bias[None, :]
    )
    input_gate = jax.nn.sigmoid(
        jnp.einsum("lhi,hij->lhj", split_in, input_weight, precision=HIGH).reshape(
            row_count, heads_local * head_width
        )
        + input_bias[None, :]
    )
    log_decay = -8.0 * rate_gate * jax.nn.softplus(-decay_param)[None, :]
    decay = jnp.exp(log_decay)
    source = jnp.sqrt(-jnp.expm1(2.0 * log_decay)) * input_gate * conv_out
    return (decay, source)


def act_piece(gate_val, up_val):
    return exact_gelu(gate_val) * up_val


def per_device(
    block_in,
    cotangent,
    norm_one,
    rec_in,
    rec_gate,
    conv_weight,
    conv_bias,
    rate_weight,
    rate_bias,
    input_weight,
    input_bias,
    decay_code,
    rec_out,
    norm_two,
    mlp_gate,
    mlp_up,
    mlp_down,
):
    gathered = (
        lax.all_gather(rec_in, "seq", axis=0, tiled=True),
        lax.all_gather(rec_gate, "seq", axis=0, tiled=True),
        lax.all_gather(rec_out, "seq", axis=1, tiled=True),
        lax.all_gather(mlp_gate, "seq", axis=0, tiled=True),
        lax.all_gather(mlp_up, "seq", axis=0, tiled=True),
        lax.all_gather(mlp_down, "seq", axis=1, tiled=True),
    )
    full_in, full_gate_rec, full_out, full_gate, full_up, full_down = gathered
    edge_len = CONV - 1
    inputs = block_in.astype(jnp.float32)
    normed_one, inv_one = norm_forward(inputs, norm_one)
    rows_one = rows_gather(normed_one)
    x_branch = dot_plain(rows_one, full_in)
    y_branch = dot_plain(rows_one, full_gate_rec)
    x_sent = x_branch.astype(jnp.bfloat16)
    group_len = x_sent.shape[0]
    edge_rows = from_behind(x_sent[group_len - edge_len :], "seq", 1)
    extended = jnp.concatenate([edge_rows, x_sent], axis=0).astype(jnp.float32)
    conv_out = conv_bias[None, :] + jnp.zeros((group_len, x_sent.shape[1]), jnp.float32)
    for offset in range(CONV):
        conv_out = (
            conv_out
            + conv_weight[offset][None, :]
            * extended[edge_len - offset : edge_len - offset + group_len]
        )
    decay_param = decay_code.astype(jnp.float32) / 256.0
    decay, source = gate_piece(
        conv_out, rate_weight, rate_bias, input_weight, input_bias, decay_param
    )
    running, local_state = lax.associative_scan(pair_combine, (decay, source), axis=0)
    channels = decay.shape[1]
    unit_vec = jnp.ones((channels,), jnp.float32)
    zero_vec = jnp.zeros((channels,), jnp.float32)
    carried = prefix(
        (running[group_len - 1], local_state[group_len - 1]),
        "seq",
        pair_combine,
        (unit_vec, zero_vec),
        False,
    )
    state_in = carried[1]
    state = local_state + running * state_in[None, :]
    y_act = exact_gelu(y_branch)
    gated = (state * y_act).astype(jnp.bfloat16)
    mixed = branch_sum(dot_plain(gated, full_out))
    resid = inputs + mixed
    normed_two, inv_two = norm_forward(resid, norm_two)
    rows_two = rows_gather(normed_two)
    gate_pre = dot_plain(rows_two, full_gate)
    up_pre = dot_plain(rows_two, full_up)
    act_rows = act_piece(gate_pre, up_pre).astype(jnp.bfloat16)
    mlp_out = branch_sum(dot_plain(act_rows, full_down))
    result = (resid + mlp_out).astype(jnp.bfloat16)
    back_weights = (
        lax.all_gather(rec_in, "seq", axis=0, tiled=True),
        lax.all_gather(rec_gate, "seq", axis=0, tiled=True),
        lax.all_gather(rec_out, "seq", axis=1, tiled=True),
        lax.all_gather(mlp_gate, "seq", axis=0, tiled=True),
        lax.all_gather(mlp_up, "seq", axis=0, tiled=True),
        lax.all_gather(mlp_down, "seq", axis=1, tiled=True),
    )
    back_in, back_gate_rec, back_out, back_gate, back_up, back_down = back_weights
    grad_top = cotangent.astype(jnp.float32)
    grad_mlp_rows = grads_gather(grad_top)
    grad_mlp_down = dot_left_t(act_rows, grad_mlp_rows)
    grad_act = dot_right_t(grad_mlp_rows, back_down)
    _, act_pull = jax.vjp(act_piece, gate_pre, up_pre)
    grad_gate_pre, grad_up_pre = act_pull(grad_act)
    grad_gate_low = grad_gate_pre.astype(jnp.bfloat16)
    grad_up_low = grad_up_pre.astype(jnp.bfloat16)
    grad_mlp_gate = dot_left_t(rows_two, grad_gate_low)
    grad_mlp_up = dot_left_t(rows_two, grad_up_low)
    grad_normed_two = feature_sum(
        dot_right_t(grad_gate_low, back_gate) + dot_right_t(grad_up_low, back_up)
    )
    grad_resid_norm, grad_norm_two = norm_backward(resid, norm_two, inv_two, grad_normed_two)
    grad_resid = grad_top + grad_resid_norm
    grad_mix_rows = grads_gather(grad_resid)
    grad_rec_out = dot_left_t(gated, grad_mix_rows)
    grad_gated = dot_right_t(grad_mix_rows, back_out)
    grad_direct = grad_gated * y_act
    _, gelu_pull = jax.vjp(exact_gelu, y_branch)
    grad_y_low = gelu_pull(grad_gated * state)[0].astype(jnp.bfloat16)
    next_decay = jnp.concatenate([decay[1:], unit_vec[None, :]], axis=0)
    after_prod, local_adj = lax.associative_scan(
        pair_combine, (next_decay, grad_direct), reverse=True, axis=0
    )
    carried_back = prefix(
        (running[group_len - 1], decay[0] * local_adj[0]),
        "seq",
        pair_combine,
        (unit_vec, zero_vec),
        True,
    )
    adjoint = local_adj + after_prod * carried_back[1][None, :]
    state_prev = jnp.concatenate([state_in[None, :], state[: group_len - 1]], axis=0)
    grad_decay = adjoint * state_prev
    _, gate_pull = jax.vjp(
        gate_piece, conv_out, rate_weight, rate_bias, input_weight, input_bias, decay_param
    )
    (
        grad_conv,
        grad_rate_weight,
        grad_rate_bias,
        grad_input_weight,
        grad_input_bias,
        grad_decay_param,
    ) = gate_pull((grad_decay, adjoint))
    grad_conv_bias = jnp.sum(grad_conv, axis=0)
    grad_conv_weight = jnp.stack(
        [
            jnp.sum(grad_conv * extended[edge_len - offset : edge_len - offset + group_len], axis=0)
            for offset in range(CONV)
        ],
        axis=0,
    )
    grad_ext = jnp.zeros_like(extended)
    for offset in range(CONV):
        grad_ext = grad_ext.at[edge_len - offset : edge_len - offset + group_len].add(
            conv_weight[offset][None, :] * grad_conv
        )
    from_next = from_behind(grad_ext[:edge_len], "seq", -1)
    grad_sent = grad_ext[edge_len:].at[group_len - edge_len :].add(from_next)
    grad_x_low = grad_sent.astype(jnp.bfloat16)
    grad_rec_in = dot_left_t(rows_one, grad_x_low)
    grad_rec_gate = dot_left_t(rows_one, grad_y_low)
    grad_normed_one = feature_sum(
        dot_right_t(grad_x_low, back_in) + dot_right_t(grad_y_low, back_gate_rec)
    )
    grad_in_norm, grad_norm_one = norm_backward(inputs, norm_one, inv_one, grad_normed_one)
    grad_input = grad_resid + grad_in_norm
    weight_sums = (
        lax.psum_scatter(
            grad_rec_in.astype(jnp.bfloat16), "seq", scatter_dimension=0, tiled=True
        ).astype(jnp.float32),
        lax.psum_scatter(
            grad_rec_gate.astype(jnp.bfloat16), "seq", scatter_dimension=0, tiled=True
        ).astype(jnp.float32),
        lax.psum_scatter(
            grad_rec_out.astype(jnp.bfloat16), "seq", scatter_dimension=1, tiled=True
        ).astype(jnp.float32),
        lax.psum_scatter(
            grad_mlp_gate.astype(jnp.bfloat16), "seq", scatter_dimension=0, tiled=True
        ).astype(jnp.float32),
        lax.psum_scatter(
            grad_mlp_up.astype(jnp.bfloat16), "seq", scatter_dimension=0, tiled=True
        ).astype(jnp.float32),
        lax.psum_scatter(
            grad_mlp_down.astype(jnp.bfloat16), "seq", scatter_dimension=1, tiled=True
        ).astype(jnp.float32),
    )
    small_sums = (
        lax.psum(grad_norm_one.astype(jnp.bfloat16), "seq").astype(jnp.float32),
        lax.psum(grad_conv_weight.astype(jnp.bfloat16), "seq").astype(jnp.float32),
        lax.psum(grad_conv_bias.astype(jnp.bfloat16), "seq").astype(jnp.float32),
        lax.psum(grad_rate_weight.astype(jnp.bfloat16), "seq").astype(jnp.float32),
        lax.psum(grad_rate_bias.astype(jnp.bfloat16), "seq").astype(jnp.float32),
        lax.psum(grad_input_weight.astype(jnp.bfloat16), "seq").astype(jnp.float32),
        lax.psum(grad_input_bias.astype(jnp.bfloat16), "seq").astype(jnp.float32),
        lax.psum(grad_decay_param.astype(jnp.bfloat16), "seq").astype(jnp.float32),
        lax.psum(grad_norm_two.astype(jnp.bfloat16), "seq").astype(jnp.float32),
    )
    return (
        result,
        grad_input,
        small_sums[0],
        weight_sums[0],
        weight_sums[1],
        small_sums[1],
        small_sums[2],
        small_sums[3],
        small_sums[4],
        small_sums[5],
        small_sums[6],
        small_sums[7],
        weight_sums[2],
        small_sums[8],
        weight_sums[3],
        weight_sums[4],
        weight_sums[5],
    )


def solution(mesh):
    return jax.shard_map(
        per_device,
        mesh=mesh,
        in_specs=(
            P("seq", "head"),
            P("seq", "head"),
            P("head"),
            P("seq", "head"),
            P("seq", "head"),
            P(None, "head"),
            P("head"),
            P("head", None, None),
            P("head"),
            P("head", None, None),
            P("head"),
            P("head"),
            P("head", "seq"),
            P("head"),
            P("seq", "head"),
            P("seq", "head"),
            P("head", "seq"),
        ),
        out_specs=(
            P("seq", "head"),
            P("seq", "head"),
            P("head"),
            P("seq", "head"),
            P("seq", "head"),
            P(None, "head"),
            P("head"),
            P("head", None, None),
            P("head"),
            P("head", None, None),
            P("head"),
            P("head"),
            P("head", "seq"),
            P("head"),
            P("seq", "head"),
            P("seq", "head"),
            P("head", "seq"),
        ),
        check_vma=False,
    )
```

profile of v0, /device:TPU:0, one launch (start us, length us, event | category | flops | bytes accessed | tf_op | source)
XLA Modules:
  0.0 2574.4 jit_solution(16232872174143473844)
XLA Ops:
  9.6 39.8 %psum.91 = f32[2048]{0:T(1024)S(1)} all-reduce(f32[2048]{0:T(1024)S(1)} %fusion.45), channel_id=1, replica_groups=mesh['seq'=8,'head'=16] {'head'}, use_global_device_ids=true, to_apply=%region_1.0 | all-reduce | flops 2048 | bytes 16384 | tf_op jit(solution)/shard_map/psum | solution.py:61
  53.0 29.7 %all_gather.48 = bf16[2048,160]{0,1:T(8,128)(2,1)S(1)} all-gather(bf16[256,160]{0,1:T(8,128)(2,1)S(1)} %copy-done.112), channel_id=1, replica_groups=mesh['seq'=8,'head'=16] {'seq'}, dimensions={0}, use_global_device_ids=true | all-gather | bytes 737280 | tf_op jit(solution)/shard_map/all_gather | solution.py:139
  82.7 31.7 %all_gather.51 = bf16[2048,160]{0,1:T(8,128)(2,1)} all-gather(bf16[256,160]{0,1:T(8,128)(2,1)S(1)} %copy-done.113), channel_id=1, replica_groups=mesh['seq'=8,'head'=16] {'seq'}, dimensions={0}, use_global_device_ids=true | all-gather | bytes 737280 | tf_op jit(solution)/shard_map/all_gather | solution.py:140
  114.4 31.5 %all_gather.52 = bf16[160,2048]{1,0:T(8,128)(2,1)} all-gather(bf16[160,256]{1,0:T(8,128)(2,1)S(1)} %copy-done.114), channel_id=1, replica_groups=mesh['seq'=8,'head'=16] {'seq'}, dimensions={1}, use_global_device_ids=true | all-gather | bytes 737280 | tf_op jit(solution)/shard_map/all_gather | solution.py:141
  164.6 23.5 slice.902
  188.2 23.4 slice.824
  211.5 23.4 slice.823
  235.6 22.9 slice.826
  258.5 22.5 slice.822
  283.6 11.7 slice.900
  295.2 11.9 slice.830
  307.1 12.2 slice.829
  320.0 12.2 slice.832
  332.2 12.2 slice.828
  344.4 12.6 slice.827
  439.6 22.5 slice.821
  513.4 11.0 pad.321
  524.4 11.2 pad.299
  535.5 11.0 pad.300
  558.2 26.6 %pad.324 = f32[2048,160]{0,1:T(8,128)} pad(f32[1024,160]{0,1:T(8,128)} %add.695, f32[]{:T(128)} %constant.266.clone.1), padding=1_0_1x0_0_0 | pad | bytes 1966084 | tf_op jit(solution)/shard_map/pad | solution.py:168
  587.8 21.6 pad.323
  610.7 19.5 all-gather
  630.3 25.0 pad.302
  655.5 24.6 pad.301
  681.2 15.6 all-gather.1
  696.9 14.0 multiply_convert_fusion.2
  720.6 141.8 %reduce-scatter.11.cloned.1.call-done = f32[2048,128]{1,0:T(8,128)} async-done(((f32[2048,2048]{1,0:T(8,128)}), f32[2048,128]{1,0:T(8,128)}) %reduce-scatter.11.cloned.1.call-update) | async-done | bytes 1048592 | tf_op jit(solution)/shard_map/reduce_scatter | solution.py:81
  864.0 33.8 %psum.92 = f32[2048]{0:T(1024)S(1)} all-reduce(f32[2048]{0:T(1024)S(1)} %get-tuple-element.326), channel_id=1, replica_groups=mesh['seq'=8,'head'=16] {'head'}, use_global_device_ids=true, to_apply=%region_6.7 | all-reduce | flops 2048 | bytes 16384 | tf_op jit(solution)/shard_map/psum | solution.py:61
  901.1 71.2 %all-gather.13.cloned.1.call-done = bf16[2048,2048]{1,0:T(8,128)(2,1)} async-done(((bf16[2048,128]{1,0:T(8,128)(2,1)}), bf16[2048,2048]{1,0:T(8,128)(2,1)}) %all-gather.13.cloned.1.call-update) | async-done | bytes 8388624 | tf_op jit(solution)/shard_map/all_gather | solution.py:77
  982.3 29.7 %all-gather.19.cloned.1.call-done = bf16[384,2048]{1,0:T(8,128)(2,1)} async-done(((bf16[384,256]{1,0:T(8,128)(2,1)}), bf16[384,2048]{1,0:T(8,128)(2,1)}) %all-gather.19.cloned.1.call-update) | async-done | bytes 1572880 | tf_op jit(solution)/shard_map/all_gather | solution.py:144
  1012.0 81.0 %all-gather.21.cloned.1.call-done = bf16[2048,2048]{1,0:T(8,128)(2,1)} async-done(((bf16[2048,128]{1,0:T(8,128)(2,1)}), bf16[2048,2048]{1,0:T(8,128)(2,1)}) %all-gather.21.cloned.1.call-update) | async-done | bytes 8388624 | tf_op jit(solution)/shard_map/all_gather | solution.py:85
  1092.9 15.8 multiply_convert_fusion
  1108.7 23.8 all-gather.17.cloned.1.call-done
  1132.5 13.7 add_convert_fusion
  1154.8 11.6 convolution_add_fusion.1
  1166.4 146.3 %reduce-scatter.15.cloned.1.call-done = f32[2048,128]{1,0:T(8,128)} async-done(((f32[2048,2048]{1,0:T(8,128)}), f32[2048,128]{1,0:T(8,128)}) %reduce-scatter.15.cloned.1.call-update) | async-done | bytes 1048592 | tf_op jit(solution)/shard_map/reduce_scatter | solution.py:89
  1315.2 33.7 %psum.93 = f32[2048]{0:T(1024)S(1)} all-reduce(f32[2048]{0:T(1024)S(1)} %get-tuple-element.280), channel_id=1, replica_groups=mesh['seq'=8,'head'=16] {'head'}, use_global_device_ids=true, to_apply=%region_10.11 | all-reduce | flops 2048 | bytes 16384 | tf_op jit(solution)/shard_map/psum | solution.py:68
  1372.5 23.5 slice.937
  1396.0 23.4 slice.930
  1419.4 23.4 slice.928
  1490.6 23.8 slice.1014
  1514.3 22.8 slice.934
  1537.1 23.4 slice.932
  1578.6 12.4 slice.1012
  1591.0 11.7 slice.942
  1602.6 12.2 slice.941
  1616.5 13.0 slice.944
  1629.5 13.2 slice.940
  1642.7 12.2 slice.939
  1845.9 11.2 pad.365
  1857.1 13.5 pad.366
  1885.3 13.5 pad.344
  1902.0 24.6 pad.345
  1926.6 26.6 %pad.346 = f32[2048,160]{0,1:T(8,128)} pad(f32[1024,160]{0,1:T(8,128)} %add.732, f32[]{:T(128)} %constant.266.clone.1), padding=1_0_1x0_0_0 | pad | bytes 1966084 | tf_op jit(solution)/shard_map/pad | solution.py:223
  1956.6 11.7 rev.8
  1968.2 18.1 all-gather.2
  1986.3 21.6 pad.367
  2008.0 26.4 %pad.368 = f32[2048,160]{0,1:T(8,128)} pad(f32[1024,160]{0,1:T(8,128)} %add.744, f32[]{:T(128)} %constant.266.clone.1), padding=1_0_1x0_0_0 | pad | bytes 1966084 | tf_op jit(solution)/shard_map/pad | solution.py:223
  2037.0 16.7 rev.9
  2162.6 20.5 reduce-scatter.19.cloned.1.call-done
  2184.6 147.8 %reduce-scatter.17.cloned.1.call-done = f32[2048,128]{1,0:T(8,128)} async-done(((f32[2048,2048]{1,0:T(8,128)}), f32[2048,128]{1,0:T(8,128)}) %reduce-scatter.17.cloned.1.call-update) | async-done | bytes 1048592 | tf_op jit(solution)/shard_map/reduce_scatter | solution.py:89
  2334.8 33.7 %psum.94 = f32[2048]{0:T(1024)S(1)} all-reduce(f32[2048]{0:T(1024)S(1)} %get-tuple-element.282), channel_id=1, replica_groups=mesh['seq'=8,'head'=16] {'head'}, use_global_device_ids=true, to_apply=%region_15.16 | all-reduce | flops 2048 | bytes 16384 | tf_op jit(solution)/shard_map/psum | solution.py:68
  2368.6 112.2 %reduce-scatter.13.cloned.1.call-done = f32[2048,128]{1,0:T(8,128)} async-done(((f32[2048,2048]{1,0:T(8,128)}), f32[2048,128]{1,0:T(8,128)}) %reduce-scatter.13.cloned.1.call-update) | async-done | bytes 1048592 | tf_op jit(solution)/shard_map/reduce_scatter | solution.py:81
  2485.0 70.2 %all-reduce.94.cloned.1.call-done = (bf16[1,160,160]{1,2,0:T(8,128)(2,1)}, bf16[1,160,160]{1,2,0:T(8,128)(2,1)}, bf16[128]{0:T(256)(128)(2,1)}, bf16[4,160]{1,0:...) async-done(((bf16[1,160,160]{1,2,0:T(8,128)(2,1)}, ...) | async-done | bytes 105488 | tf_op jit(solution)/shard_map/psum | solution.py:294
  (728 shorter events, 651.3 us)
Async XLA Ops:
  8.0 151.4 %copy-start = (f32[1,160,160]{2,1,0:T(8,128)S(1)}, f32[1,160,160]{2,1,0:T(8,128)}, u32[]{:S(2)}) copy-start(f32[1,160,160]{2,1,0:T(8,128)} %param.40) | copy-start | bytes 307204
  8.0 44.3 %copy-start.133 = (s32[160]{0:T(256)S(1)}, s32[160]{0:T(256)}, u32[]{:S(2)}) copy-start(s32[160]{0:T(256)} %param.42) | copy-start | bytes 1924
  8.0 44.9 %copy-start.135 = (f32[4,160]{1,0:T(4,128)S(1)}, f32[4,160]{1,0:T(4,128)}, u32[]{:S(2)}) copy-start(f32[4,160]{1,0:T(4,128)} %param.36) | copy-start | bytes 7684
  8.1 44.9 %copy-start.112 = (bf16[256,160]{0,1:T(8,128)(2,1)S(1)}, bf16[256,160]{0,1:T(8,128)(2,1)}, u32[]{:S(2)}) copy-start(bf16[256,160]{0,1:T(8,128)(2,1)} %param.34) | copy-start | bytes 245764
  8.1 137.8 %all-gather.11.cloned.1.call-start = ((), (), s32[]{:S(2)}) async-start(), calls=%async_computation.10 | async-start | bytes 8912896 | tf_op jit(solution)/shard_map/all_gather | solution.py:77
  9.5 73.1 %copy-start.113 = (bf16[256,160]{0,1:T(8,128)(2,1)S(1)}, bf16[256,160]{0,1:T(8,128)(2,1)}, u32[]{:S(2)}) copy-start(bf16[256,160]{0,1:T(8,128)(2,1)} %param.35) | copy-start | bytes 245764
  50.0 64.3 %copy-start.114 = (bf16[160,256]{1,0:T(8,128)(2,1)S(1)}, bf16[160,256]{1,0:T(8,128)(2,1)}, u32[]{:S(2)}) copy-start(bf16[160,256]{1,0:T(8,128)(2,1)} %param.43) | copy-start | bytes 245764
  52.3 810.1 %reduce-scatter.11.cloned.1.call-start = ((), (), s32[]{:S(2)}) async-start(), calls=%async_computation.11 | async-start | bytes 17825792 | tf_op jit(solution)/shard_map/reduce_scatter | solution.py:81
  52.9 106.5 %copy-start.126 = (f32[160]{0:T(256)}, f32[160]{0:T(256)S(1)}, u32[]{:S(2)}) copy-start(f32[160]{0:T(256)S(1)} %get-tuple-element.331) | copy-start | bytes 1924
  52.9 103.5 %copy-start.118 = (f32[1,160]{1,0:T(1,128)}, f32[1,160]{1,0:T(1,128)S(1)}, u32[]{:S(2)}) copy-start(f32[1,160]{1,0:T(1,128)S(1)} %get-tuple-element.441) | copy-start | bytes 1924
  52.9 103.5 %copy-start.120 = (f32[1,160]{1,0:T(1,128)}, f32[1,160]{1,0:T(1,128)S(1)}, u32[]{:S(2)}) copy-start(f32[1,160]{1,0:T(1,128)S(1)} %get-tuple-element.442) | copy-start | bytes 1924
  53.0 103.5 %copy-start.122 = (f32[1,160]{1,0:T(1,128)}, f32[1,160]{1,0:T(1,128)S(1)}, u32[]{:S(2)}) copy-start(f32[1,160]{1,0:T(1,128)S(1)} %get-tuple-element.440) | copy-start | bytes 1924
  53.0 103.5 %copy-start.124 = (f32[1,160]{1,0:T(1,128)}, f32[1,160]{1,0:T(1,128)S(1)}, u32[]{:S(2)}) copy-start(f32[1,160]{1,0:T(1,128)S(1)} %get-tuple-element.439) | copy-start | bytes 1924
  82.7 69.5 %copy-start.28 = (bf16[2048,160]{0,1:T(8,128)(2,1)}, bf16[2048,160]{0,1:T(8,128)(2,1)S(1)}, u32[]{:S(2)}) copy-start(bf16[2048,160]{0,1:T(8,128)(2,1)S(1)} %all_gather.48) | copy-start | bytes 1966084
  152.2 3.9 collective-permute-start
  162.9 276.6 %copy-start.16 = (f32[2048,160]{0,1:T(8,128)}, f32[2048,160]{0,1:T(8,128)S(1)}, u32[]{:S(2)}) copy-start(f32[2048,160]{0,1:T(8,128)S(1)} %get-tuple-element.342) | copy-start | bytes 3932164
  439.6 22.6 copy-start.106
  439.6 23.9 copy-start.105
  439.6 24.1 copy-start.90
  439.6 24.1 copy-start.91
  513.4 33.1 %copy-start.67 = (f32[512,160]{0,1:T(8,128)S(1)}, f32[512,160]{0,1:T(8,128)}, u32[]{:S(2)}) copy-start(f32[512,160]{0,1:T(8,128)} %add.694) | copy-start | bytes 983044
  587.8 42.5 %copy-start.40 = (f32[1024,160]{0,1:T(8,128)S(1)}, f32[1024,160]{0,1:T(8,128)}, u32[]{:S(2)}) copy-start(f32[1024,160]{0,1:T(8,128)} %add.683) | copy-start | bytes 1966084
  609.4 46.0 %copy-start.62 = (f32[2048,160]{0,1:T(8,128)}, f32[2048,160]{0,1:T(8,128)S(1)}, u32[]{:S(2)}) copy-start(f32[2048,160]{0,1:T(8,128)S(1)} %pad.323) | copy-start | bytes 3932164
  609.4 45.8 %copy-start.35 = (f32[1023,160]{0,1:T(8,128)S(1)}, f32[1023,160]{0,1:T(8,128)}, u32[]{:S(2)}) copy-start(f32[1023,160]{0,1:T(8,128)} %get-tuple-element.351) | copy-start | bytes 1964164
  609.5 45.8 %copy-start.98 = (f32[1,160]{0,1:T(8,128)S(1)}, f32[1,160]{0,1:T(8,128)}, u32[]{:S(2)}) copy-start(f32[1,160]{0,1:T(8,128)} %slice.1049) | copy-start | bytes 1924
  655.5 41.4 %copy-start.30 = (bf16[2048,160]{0,1:T(8,128)(2,1)S(1)}, bf16[2048,160]{0,1:T(8,128)(2,1)}, u32[]{:S(2)}) copy-start(bf16[2048,160]{0,1:T(8,128)(2,1)} %all_gather.51) | copy-start | bytes 1966084
  719.9 142.5 %copy-start.4 = (bf16[2048,128]{1,0:T(8,128)(2,1)S(1)}, bf16[2048,128]{1,0:T(8,128)(2,1)}, u32[]{:S(2)}) copy-start(bf16[2048,128]{1,0:T(8,128)(2,1)} %param.31) | copy-start | bytes 1572868
  719.9 181.1 %all-gather.15.cloned.1.call-start = ((), (), s32[]{:S(2)}) async-start(), calls=%async_computation.13 | async-start | bytes 1769472 | tf_op jit(solution)/shard_map/all_gather | solution.py:142
  720.5 177.2 %copy-start.131 = (f32[128]{0:T(128)S(1)}, f32[128]{0:T(128)}, u32[]{:S(2)}) copy-start(f32[128]{0:T(128)} %param.44) | copy-start | bytes 1540
  720.5 251.7 %all-gather.13.cloned.1.call-start = ((), (), s32[]{:S(2)}) async-start(), calls=%async_computation.12 | async-start | bytes 8912896 | tf_op jit(solution)/shard_map/all_gather | solution.py:77
  898.9 113.1 %all-gather.19.cloned.1.call-start = ((), (), s32[]{:S(2)}) async-start(), calls=%async_computation.15 | async-start | bytes 1769472 | tf_op jit(solution)/shard_map/all_gather | solution.py:144
  899.5 193.5 %all-gather.21.cloned.1.call-start = ((), (), s32[]{:S(2)}) async-start(), calls=%async_computation.17 | async-start | bytes 8912896 | tf_op jit(solution)/shard_map/all_gather | solution.py:85
  900.2 232.2 %all-gather.17.cloned.1.call-start = ((), (), s32[]{:S(2)}) async-start(), calls=%async_computation.14 | async-start | bytes 1769472 | tf_op jit(solution)/shard_map/all_gather | solution.py:143
  901.0 411.8 %reduce-scatter.15.cloned.1.call-start = ((), (), s32[]{:S(2)}) async-start(), calls=%async_computation.18 | async-start | bytes 17825792 | tf_op jit(solution)/shard_map/reduce_scatter | solution.py:89
  1108.7 46.1 %copy-start.23 = (bf16[2048,384]{1,0:T(8,128)(2,1)}, bf16[2048,384]{1,0:T(8,128)(2,1)S(1)}, u32[]{:S(2)}) copy-start(bf16[2048,384]{1,0:T(8,128)(2,1)S(1)} %get-tuple-element.324) | copy-start | bytes 4718596
  1166.4 182.6 %copy-start.20 = (bf16[2048,128]{1,0:T(8,128)(2,1)S(1)}, bf16[2048,128]{1,0:T(8,128)(2,1)}, u32[]{:S(2)}) copy-start(bf16[2048,128]{1,0:T(8,128)(2,1)} %param.32) | copy-start | bytes 1572868
  1166.4 313.7 %all-gather.23.cloned.1.call-start = ((), (), s32[]{:S(2)}) async-start(), calls=%async_computation.19 | async-start | bytes 8912896 | tf_op jit(solution)/shard_map/all_gather | solution.py:85
  1312.7 36.2 %copy-start.14 = (f32[2048,128]{1,0:T(8,128)S(1)}, f32[2048,128]{1,0:T(8,128)}, u32[]{:S(2)}) copy-start(f32[2048,128]{1,0:T(8,128)} %reduce-scatter.15.cloned.1.call-done) | copy-start | bytes 3145732
  1350.4 797.5 %reduce-scatter.29.cloned.1.call-start = ((), (), s32[]{:S(2)}) async-start(), calls=%async_computation.26 | async-start | bytes 1769472 | tf_op jit(solution)/shard_map/reduce_scatter | solution.py:286
  1359.0 790.7 %reduce-scatter.25.cloned.1.call-start = ((), (), s32[]{:S(2)}) async-start(), calls=%async_computation.24 | async-start | bytes 1769472 | tf_op jit(solution)/shard_map/reduce_scatter | solution.py:280
  1369.6 781.8 %reduce-scatter.27.cloned.1.call-start = ((), (), s32[]{:S(2)}) async-start(), calls=%async_computation.25 | async-start | bytes 1769472 | tf_op jit(solution)/shard_map/reduce_scatter | solution.py:283
  1480.0 679.5 %reduce-scatter.23.cloned.1.call-start = ((), (), s32[]{:S(2)}) async-start(), calls=%async_computation.23 | async-start | bytes 737280 | tf_op jit(solution)/shard_map/reduce_scatter | solution.py:277
  1614.9 27.9 %copy-start.22 = (f32[1024,160]{0,1:T(8,128)S(1)}, f32[1024,160]{0,1:T(8,128)}, u32[]{:S(2)}) copy-start(f32[1024,160]{0,1:T(8,128)} %get-tuple-element.350) | copy-start | bytes 1966084
  1800.2 16.4 copy-start.71
  2036.9 21.9 copy-start.2
  2036.9 21.9 copy-start.107
  2036.9 21.9 copy-start.119
  2036.9 21.9 copy-start.121
  2036.9 21.9 copy-start.123
  2036.9 21.9 copy-start.125
  2036.9 21.9 copy-start.127
  2037.0 21.9 copy-start.129
  2073.0 88.0 %reduce-scatter.21.cloned.1.call-start = ((), (), s32[]{:S(2)}) async-start(), calls=%async_computation.22 | async-start | bytes 737280 | tf_op jit(solution)/shard_map/reduce_scatter | solution.py:274
  2087.5 95.6 %reduce-scatter.19.cloned.1.call-start = ((), (), s32[]{:S(2)}) async-start(), calls=%async_computation.21 | async-start | bytes 737280 | tf_op jit(solution)/shard_map/reduce_scatter | solution.py:271
  2110.4 7.2 collective-permute-start.1
  2124.9 207.5 %reduce-scatter.17.cloned.1.call-start = ((), (), s32[]{:S(2)}) async-start(), calls=%async_computation.20 | async-start | bytes 17825792 | tf_op jit(solution)/shard_map/reduce_scatter | solution.py:89
  2136.9 343.9 %reduce-scatter.13.cloned.1.call-start = ((), (), s32[]{:S(2)}) async-start(), calls=%async_computation.16 | async-start | bytes 17825792 | tf_op jit(solution)/shard_map/reduce_scatter | solution.py:81
  2147.8 407.4 %all-reduce.94.cloned.1.call-start = ((), (), s32[]{:S(2)}) async-start(), calls=%async_computation.27 | async-start | bytes 337920 | tf_op jit(solution)/shard_map/psum | solution.py:294
  2157.0 175.4 %copy-start.5 = (bf16[2048,128]{1,0:T(8,128)(2,1)S(1)}, bf16[2048,128]{1,0:T(8,128)(2,1)}, u32[]{:S(2)}) copy-start(bf16[2048,128]{1,0:T(8,128)(2,1)} %param.31) | copy-start | bytes 1572868
  2157.0 175.4 %copy-start.111 = (f32[2048]{0:T(1024)S(1)}, f32[2048]{0:T(1024)}, u32[]{:S(2)}) copy-start(f32[2048]{0:T(1024)} %copy-done.110) | copy-start | bytes 24580
  2157.0 175.4 %copy-start.132 = (f32[128]{0:T(128)S(1)}, f32[128]{0:T(128)}, u32[]{:S(2)}) copy-start(f32[128]{0:T(128)} %param.33) | copy-start | bytes 1540
  2158.9 209.7 %copy-start.116 = (f32[2048]{0:T(1024)S(1)}, f32[2048]{0:T(1024)}, u32[]{:S(2)}) copy-start(f32[2048]{0:T(1024)} %copy-done.115) | copy-start | bytes 24580
  2158.9 321.9 %copy-start.15 = (f32[2048,128]{1,0:T(8,128)S(1)}, f32[2048,128]{1,0:T(8,128)}, u32[]{:S(2)}) copy-start(f32[2048,128]{1,0:T(8,128)} %reduce-scatter.15.cloned.1.call-done) | copy-start | bytes 3145732
  2158.9 321.9 %copy-start.21 = (bf16[2048,128]{1,0:T(8,128)(2,1)S(1)}, bf16[2048,128]{1,0:T(8,128)(2,1)}, u32[]{:S(2)}) copy-start(bf16[2048,128]{1,0:T(8,128)(2,1)} %param.32) | copy-start | bytes 1572868
  (96 other events, 459.0 us)
Sparse Core Ops, SparseCore 0:
  52.4 81.4 all-gather.10
  720.1 142.2 reduce-scatter.10
  1350.5 82.2 all-gather.22
Sparse Core Ops, SparseCore 1:
  722.0 36.1 all-gather.14
  899.0 73.2 all-gather.12
  973.7 38.2 all-gather.18
  1014.3 78.5 all-gather.20
  1094.6 37.8 all-gather.16
  1166.5 146.2 reduce-scatter.14
  1359.1 37.1 reduce-scatter.28
  1398.5 39.6 reduce-scatter.24
  1480.0 37.0 reduce-scatter.26
  2073.0 31.3 reduce-scatter.22
  2106.7 37.0 reduce-scatter.20
  2146.2 36.8 reduce-scatter.18
  2187.2 145.1 reduce-scatter.16
  2336.7 144.0 reduce-scatter.12
  2485.2 70.1 all-reduce.93
where the time goes:
time: 2590 us; the launch traced here: 2570 us
  local copies, waits for them, and re-layouts  1110 us (43%)
  waiting for transfers between devices  853 us (33%)
  blocking collectives  287 us (11%)
  matrix products  177 us (7%)
  other arithmetic  125 us (5%)
    slice x69, local copies, waits for them, and re-layouts, per_device(): lax.associative_scan(pair_combine, (next_decay, grad_direct), reverse=Tru...  338 us
    reduce_scatter x2, waiting for transfers between devices, feature_sum(): lax.psum_scatter(partial_rows, 'head', scatter_dimension=1, tiled=True)  294 us
    slice x66, local copies, waits for them, and re-layouts, per_device(): lax.associative_scan(pair_combine, (decay, source), axis=0)  293 us
    reduce_scatter x2, waiting for transfers between devices, branch_sum(): lax.psum_scatter(partial_rows, 'head', scatter_dimension=1, tiled=True)  254 us
    pad x40, local copies, waits for them, and re-layouts, per_device(): lax.associative_scan(pair_combine, (next_decay, grad_direct), reverse=Tru...  209 us
    pad x40, local copies, waits for them, and re-layouts, per_device(): lax.associative_scan(pair_combine, (decay, source), axis=0)  187 us
    all_gather x2, waiting for transfers between devices, grads_gather(): lax.all_gather(grad_rows.astype(jnp.bfloat16), 'head', axis=1, tiled=True)  81 us
    psum x2, blocking collectives, norm_forward(): summed = lax.psum(jnp.sum(values * values, axis=1), 'head')  73.6 us
  transfers between devices with their start and end apart: 20, of which 12 were waited for; matrix products, arithmetic and copies ran while one was open for 32% of the time, Pallas kernels for 0%

commit v1 on v0

v1 whole, which is shorter than its diff:
```python
import jax
import jax.numpy as jnp
from jax import lax
from jax.experimental import pallas as pl
from jax.experimental.pallas import tpu as pltpu
from jax.sharding import Mesh, PartitionSpec as P

D = 2048
CONV = 4
EPS = 1e-06
TOK = 512
CH = 640
HW = 160
MESH = pl.DeviceIdType.MESH
SEQ = ("ylo", "x")
HEAD = ("z", "yhi", "core")
QUAD = ("yhi", "core")
PLANE = ("ylo", "x", "yhi", "core")
bf = jnp.bfloat16
f32 = jnp.float32
VMEM = pl.BlockSpec(memory_space=pltpu.VMEM)


def shape(dims, dtype):
    return jax.ShapeDtypeStruct(dims, dtype)


def params(cid):
    return pltpu.CompilerParams(
        collective_id=cid, has_side_effects=True, vmem_limit_bytes=56 * 2**20
    )


def quad_device(index):
    return {"yhi": index // 2, "core": lax.rem(index, 2)}


def plane_device(block):
    return {
        "ylo": block // 16,
        "x": lax.rem(block // 4, 4),
        "yhi": lax.rem(block // 2, 2),
        "core": lax.rem(block, 2),
    }


def meet(devices):
    barrier = pltpu.get_barrier_semaphore()
    for device in devices:
        pl.semaphore_signal(barrier, inc=1, device_id=device, device_id_type=MESH)
    pl.semaphore_wait(barrier, len(devices))


def ring_gather(full, width, send, recv, base):
    z = lax.axis_index("z")
    right, left = lax.rem(z + 1, 4), lax.rem(z + 3, 4)
    half = full.shape[0] // 2

    def part(row, block):
        return full.at[pl.ds(row, half), pl.ds(pl.multiple_of(block * width, 128), width)]

    def start(i, row, block, to):
        copy = pltpu.make_async_remote_copy(
            src_ref=part(row, block),
            dst_ref=part(row, block),
            send_sem=send.at[base + i],
            recv_sem=recv.at[base + i],
            device_id={"z": to},
            device_id_type=MESH,
        )
        copy.start()
        return copy

    c0 = start(0, 0, z, right)
    c1 = start(1, half, z, left)
    c2 = start(2, half, z, right)
    c3 = start(3, 0, z, left)
    c0.wait_recv()
    c4 = start(4, 0, left, right)
    c1.wait_recv()
    c5 = start(5, half, right, left)
    for copy in (c2, c3, c4, c5):
        copy.wait_recv()
    for copy in (c0, c1, c2, c3, c4, c5):
        copy.wait_send()


def ring_sum(part, out, got, sent, send, recv, base):
    z = lax.axis_index("z")
    right, left, far = lax.rem(z + 1, 4), lax.rem(z + 3, 4), lax.rem(z + 2, 4)
    half = part.shape[0] // 2
    width = part.shape[1] // 4
    lo, hi = pl.ds(0, half), pl.ds(half, half)

    def cols(block):
        return pl.ds(pl.multiple_of(block * width, 128), width)

    def start(i, source, to):
        copy = pltpu.make_async_remote_copy(
            src_ref=source,
            dst_ref=got.at[i],
            send_sem=send.at[base + i],
            recv_sem=recv.at[base + i],
            device_id={"z": to},
            device_id_type=MESH,
        )
        copy.start()
        return copy

    c0 = start(0, part.at[lo, cols(far)], right)
    c1 = start(1, part.at[hi, cols(far)], left)
    c2 = start(2, part.at[hi, cols(right)], right)
    c3 = start(3, part.at[lo, cols(left)], left)
    c0.wait_recv()
    sent[0] = (got[0].astype(f32) + part[lo, cols(right)].astype(f32)).astype(bf)
    c4 = start(4, sent.at[0], right)
    c1.wait_recv()
    sent[1] = (got[1].astype(f32) + part[hi, cols(left)].astype(f32)).astype(bf)
    c5 = start(5, sent.at[1], left)
    c3.wait_recv()
    c4.wait_recv()
    out[lo, :] = part[lo, cols(z)].astype(f32) + got[3].astype(f32) + got[4].astype(f32)
    c2.wait_recv()
    c5.wait_recv()
    out[hi, :] = part[hi, cols(z)].astype(f32) + got[2].astype(f32) + got[5].astype(f32)
    for copy in (c0, c1, c2, c3, c4, c5):
        copy.wait_send()


def z_others():
    z = lax.axis_index("z")
    return [{"z": lax.rem(z + j, 4)} for j in (1, 2, 3)]


def quad_others():
    me = lax.axis_index("yhi") * 2 + lax.axis_index("core")
    return [quad_device(lax.rem(me + j, 4)) for j in (1, 2, 3)]


def quad_gather_tokens(tokens, full, send, recv, base):
    z = lax.axis_index("z")
    me = lax.axis_index("yhi") * 2 + lax.axis_index("core")
    mine = pl.ds(pl.multiple_of(z * 512 + me * 128, 128), 128)
    copies = []
    for j in (1, 2, 3):
        peer = lax.rem(me + j, 4)
        copy = pltpu.make_async_remote_copy(
            src_ref=tokens.at[pl.ds(pl.multiple_of(peer * TOK, TOK), TOK), :],
            dst_ref=full.at[:, mine],
            send_sem=send.at[base + j - 1],
            recv_sem=recv.at[base + j - 1],
            device_id=quad_device(peer),
            device_id_type=MESH,
        )
        copy.start()
        copies.append(copy)
    full[:, mine] = tokens[pl.ds(pl.multiple_of(me * TOK, TOK), TOK), :]
    return copies


def entry_kernel(
    tokens, rate_w, input_w, vectors, norms,
    full, rate_all, input_all, vectors_all, norms_all,
    send, recv,
):
    z = lax.axis_index("z")
    me = lax.axis_index("yhi") * 2 + lax.axis_index("core")
    meet(quad_others() + z_others())
    copies = quad_gather_tokens(tokens, full, send, recv, 0)
    small = []
    for k, (source, target) in enumerate(
        (
            (norms, norms_all.at[z, me]),
            (vectors, vectors_all.at[me]),
            (rate_w, rate_all.at[me]),
            (input_w, input_all.at[me]),
        )
    ):
        for j in (1, 2, 3):
            copy = pltpu.make_async_remote_copy(
                src_ref=source,
                dst_ref=target,
                send_sem=send.at[9 + 3 * k + j - 1],
                recv_sem=recv.at[9 + 3 * k + j - 1],
                device_id=quad_device(lax.rem(me + j, 4)),
                device_id_type=MESH,
            )
            copy.start()
            small.append(copy)
    norms_all[z, me] = norms[...]
    vectors_all[me] = vectors[...]
    rate_all[me] = rate_w[...]
    input_all[me] = input_w[...]
    for copy in copies:
        copy.wait_recv()
    for copy in small[:3]:
        copy.wait_recv()
    for j in (1, 2, 3):
        copy = pltpu.make_async_remote_copy(
            src_ref=norms_all.at[z],
            dst_ref=norms_all.at[z],
            send_sem=send.at[21 + j - 1],
            recv_sem=recv.at[21 + j - 1],
            device_id={"z": lax.rem(z + j, 4)},
            device_id_type=MESH,
        )
        copy.start()
        small.append(copy)
    ring_gather(full, 512, send, recv, 3)
    for copy in small[3:]:
        copy.wait_recv()
    for copy in copies + small:
        copy.wait_send()


def entry(tokens, rate_w, input_w, vectors, norms):
    return pl.pallas_call(
        entry_kernel,
        out_shape=(
            shape((TOK, D), bf),
            shape((4, HW, HW), f32),
            shape((4, HW, HW), f32),
            shape((4, 16, HW), f32),
            shape((4, 4, 8, 128), f32),
        ),
        in_specs=[VMEM] * 5,
        out_specs=[VMEM] * 5,
        scratch_shapes=[pltpu.SemaphoreType.DMA((24,)), pltpu.SemaphoreType.DMA((24,))],
        compiler_params=params(0),
        name="entry",
    )(tokens, rate_w, input_w, vectors, norms)


def gather_kernel(tokens, full, send, recv):
    meet(quad_others() + z_others())
    copies = quad_gather_tokens(tokens, full, send, recv, 0)
    for copy in copies:
        copy.wait_recv()
    ring_gather(full, 512, send, recv, 3)
    for copy in copies:
        copy.wait_send()


def gather_tokens(tokens):
    return pl.pallas_call(
        gather_kernel,
        out_shape=shape((TOK, D), bf),
        in_specs=[VMEM],
        out_specs=VMEM,
        scratch_shapes=[pltpu.SemaphoreType.DMA((9,)), pltpu.SemaphoreType.DMA((9,))],
        compiler_params=params(1),
        name="gather_tokens",
    )(tokens)


def allsum_kernel(part, full, own, got, sent, send, recv):
    z = lax.axis_index("z")
    meet(z_others())
    ring_sum(part, own, got, sent, send, recv, 0)
    full[:, pl.ds(pl.multiple_of(z * 512, 128), 512)] = own[...].astype(bf)
    ring_gather(full, 512, send, recv, 6)


def allsum(part):
    return pl.pallas_call(
        allsum_kernel,
        out_shape=(shape((TOK, D), bf), shape((TOK, 512), f32)),
        in_specs=[VMEM],
        out_specs=[VMEM] * 2,
        scratch_shapes=[
            pltpu.VMEM((6, TOK // 2, 512), bf),
            pltpu.VMEM((2, TOK // 2, 512), bf),
            pltpu.SemaphoreType.DMA((12,)),
            pltpu.SemaphoreType.DMA((12,)),
        ],
        compiler_params=params(2),
        name="allsum",
    )(part)


def sum_kernel(part, own, got, sent, send, recv):
    meet(z_others())
    ring_sum(part, own, got, sent, send, recv, 0)


def ownsum(part):
    return pl.pallas_call(
        sum_kernel,
        out_shape=shape((TOK, 512), f32),
        in_specs=[VMEM],
        out_specs=VMEM,
        scratch_shapes=[
            pltpu.VMEM((6, TOK // 2, 512), bf),
            pltpu.VMEM((2, TOK // 2, 512), bf),
            pltpu.SemaphoreType.DMA((6,)),
            pltpu.SemaphoreType.DMA((6,)),
        ],
        compiler_params=params(3),
        name="ownsum",
    )(part)


def line_devices():
    ylo, x = lax.axis_index("ylo"), lax.axis_index("x")
    row = ylo * 4 + x
    rows = [
        {"ylo": lax.rem(row + j, 8) // 4, "x": lax.rem(row + j, 4)} for j in range(1, 8)
    ]
    return quad_others() + rows


def my_block():
    row = lax.axis_index("ylo") * 4 + lax.axis_index("x")
    return row * 4 + lax.axis_index("yhi") * 2 + lax.axis_index("core")


def line_prefix(mine, quad, rows, total, send, recv, base, backward):
    me = lax.axis_index("yhi") * 2 + lax.axis_index("core")
    row = lax.axis_index("ylo") * 4 + lax.axis_index("x")
    copies = []
    for j in (1, 2, 3):
        copy = pltpu.make_async_remote_copy(
            src_ref=mine,
            dst_ref=quad.at[me],
            send_sem=send.at[base + j - 1],
            recv_sem=recv.at[base + j - 1],
            device_id=quad_device(lax.rem(me + j, 4)),
            device_id_type=MESH,
        )
        copy.start()
        copies.append(copy)
    quad[me] = mine[...]
    for copy in copies:
        copy.wait_recv()
    ones = jnp.ones((1, CH), f32)
    zeros = jnp.zeros((1, CH), f32)
    prod, end, prod_all, end_all = ones, zeros, ones, zeros
    for turn in range(4):
        q = 3 - turn if backward else turn
        a, b = quad[q, 0:1, :], quad[q, 1:2, :]
        end_all = a * end_all + b
        prod_all = a * prod_all
        take = (q > me) if backward else (q < me)
        end = jnp.where(take, a * end + b, end)
        prod = jnp.where(take, a * prod, prod)
    total[0:1, :] = prod_all
    total[1:2, :] = end_all
    for j in range(1, 8):
        other = lax.rem(row + j, 8)
        copy = pltpu.make_async_remote_copy(
            src_ref=total,
            dst_ref=rows.at[row],
            send_sem=send.at[base + 2 + j],
            recv_sem=recv.at[base + 2 + j],
            device_id={"ylo": other // 4, "x": lax.rem(other, 4)},
            device_id_type=MESH,
        )
        copy.start()
        copies.append(copy)
    rows[row] = total[...]
    for copy in copies[3:]:
        copy.wait_recv()
    came = zeros
    for turn in range(8):
        r = 7 - turn if backward else turn
        a, b = rows[r, 0:1, :], rows[r, 1:2, :]
        take = (r > row) if backward else (r < row)
        came = jnp.where(take, a * came + b, came)
    for copy in copies:
        copy.wait_send()
    return prod * came + end


def split(values):
    high = values.astype(bf)
    return high, (values - high.astype(f32)).astype(bf)


def dot3(a, b, dims):
    (ah, al), (bh, bl) = a, b

    def one(p, q):
        return lax.dot_general(p, q, (dims, ((), ())), preferred_element_type=f32)

    return one(ah, bh) + (one(al, bh) + one(ah, bl))


def minus_expm1(v):
    near = -v * (
        1.0
        + v * (1 / 2) * (1.0 + v * (1 / 3) * (1.0 + v * (1 / 4) * (1.0 + v * (1 / 5) * (1.0 + v * (1 / 6)))))
    )
    return jnp.where(v > -0.3, near, 1.0 - jnp.exp(v))


def gelu_parts(v):
    cdf = 0.5 * (1.0 + lax.erf(v * 0.7071067811865476))
    pdf = 0.3989422804014327 * jnp.exp(-0.5 * v * v)
    return v * cdf, cdf + v * pdf


def shifted(values, by, fill, reverse):
    rows = lax.broadcasted_iota(jnp.int32, values.shape, 0)
    size = values.shape[0]
    if reverse:
        return jnp.where(rows < size - by, pltpu.roll(values, size - by, 0), fill)
    return jnp.where(rows >= by, pltpu.roll(values, by, 0), fill)


def behind(near, by):
    return near[8:24, :] if by == 0 else pltpu.roll(near, by, 0)[8:24, :]


def ahead(near, by):
    size = near.shape[0]
    return pltpu.roll(near, size - by, 0)[0 : size - 8, :]


def scan8(a, b, reverse):
    for by in (1, 2, 4):
        b = b + a * shifted(b, by, 0.0, reverse)
        a = a * shifted(a, by, 1.0, reverse)
    return a, b


def loop(count, body):
    def one(i, carry):
        body(i)
        return carry

    lax.fori_loop(0, count, one, 0)


def forward_kernel(
    xs, yb, gate_hi, gate_lo, vec,
    c, rate, gin, a, m, h, hy, ext, state_in, total_a,
    halo, pre, prod, mine, quad, rows, total, send, recv,
):
    block = my_block()
    after, before = lax.rem(block + 1, 32), lax.rem(block + 31, 32)
    meet(line_devices() + [plane_device(after), plane_device(before)])
    edge = pltpu.make_async_remote_copy(
        src_ref=xs.at[pl.ds(TOK - 16, 16), :],
        dst_ref=halo,
        send_sem=send.at[10],
        recv_sem=recv.at[10],
        device_id=plane_device(after),
        device_id_type=MESH,
    )
    edge.start()

    def widen(i):
        ext[pl.ds(pl.multiple_of(8 + i * 16, 8), 16), :] = xs[
            pl.ds(pl.multiple_of(i * 16, 16), 16), :
        ].astype(f32)

    loop(TOK // 16, widen)
    edge.wait_recv()
    ext[0:8, :] = jnp.where(block > 0, halo[8:16, :].astype(f32), 0.0)

    def conv(i):
        r = i * 16
        near = ext[pl.ds(pl.multiple_of(r, 16), 24), :]
        acc = vec[4:5, :] + vec[0:1, :] * near[8:24, :]
        for k in (1, 2, 3):
            acc = acc + vec[k : k + 1, :] * behind(near, k)
        c[pl.ds(pl.multiple_of(r, 16), 16), :] = acc

    loop(TOK // 16, conv)

    def gates(i):
        r = pl.ds(pl.multiple_of(i * 128, 128), 128)
        pre[r, :] = dot3(split(c[r, :]), (gate_hi[...], gate_lo[...]), ((1,), (0,)))

    loop(TOK // 128, gates)

    def point(i, carry):
        prod_in, state = carry
        r = pl.ds(pl.multiple_of(i * 8, 8), 8)
        rr = jax.nn.sigmoid(pre[r, 0:CH] + vec[5:6, :])
        gg = jax.nn.sigmoid(pre[r, CH:] + vec[6:7, :])
        log_a = -8.0 * rr * vec[7:8, :]
        aa = jnp.exp(log_a)
        mm = jnp.sqrt(minus_expm1(2.0 * log_a))
        rate[r, :] = rr
        gin[r, :] = gg
        a[r, :] = aa
        m[r, :] = mm
        pa, hb = scan8(aa, mm * gg * c[r, :], False)
        hb = hb + pa * state
        pa = pa * prod_in
        h[r, :] = hb
        prod[r, :] = pa
        return pa[7:8, :], hb[7:8, :]

    last = lax.fori_loop(
        0, TOK // 8, point, (jnp.ones((1, CH), f32), jnp.zeros((1, CH), f32))
    )
    mine[...] = jnp.zeros((8, CH), f32)
    total[...] = jnp.zeros((8, CH), f32)
    mine[0:1, :] = last[0]
    mine[1:2, :] = last[1]
    came = line_prefix(mine, quad, rows, total, send, recv, 0, False)
    state_in[...] = jnp.broadcast_to(came, (8, CH))
    total_a[...] = jnp.broadcast_to(last[0], (8, CH))

    def finish(i):
        r = pl.ds(pl.multiple_of(i * 16, 16), 16)
        hh = h[r, :] + prod[r, :] * came
        h[r, :] = hh
        hy[r, :] = (hh * gelu_parts(yb[r, :])[0]).astype(bf)

    loop(TOK // 16, finish)
    edge.wait_send()


def forward_scan(xs, yb, gate_hi, gate_lo, vec):
    wide = shape((TOK, CH), f32)
    return pl.pallas_call(
        forward_kernel,
        out_shape=(
            wide, wide, wide, wide, wide, wide,
            shape((TOK, CH), bf),
            shape((TOK + 8, CH), f32),
            shape((8, CH), f32),
            shape((8, CH), f32),
        ),
        in_specs=[VMEM] * 5,
        out_specs=[VMEM] * 10,
        scratch_shapes=[
            pltpu.VMEM((16, CH), bf),
            pltpu.VMEM((TOK, 2 * CH), f32),
            pltpu.VMEM((TOK, CH), f32),
            pltpu.VMEM((8, CH), f32),
            pltpu.VMEM((4, 8, CH), f32),
            pltpu.VMEM((8, 8, CH), f32),
            pltpu.VMEM((8, CH), f32),
            pltpu.SemaphoreType.DMA((11,)),
            pltpu.SemaphoreType.DMA((11,)),
        ],
        compiler_params=params(4),
        name="forward_scan",
    )(xs, yb, gate_hi, gate_lo, vec)


def backward_kernel(
    dhy, yb, gate_hi, gate_lo, vec, c, rate, gin, a, m, h, ext, state_in, total_a,
    dxb, dyb, dgate, sums,
    e, apad, hpad, q, prod, pri, dc, halo, mine, quad, rows, total, send, recv,
):
    block = my_block()
    after, before = lax.rem(block + 1, 32), lax.rem(block + 31, 32)
    meet(line_devices() + [plane_device(after), plane_device(before)])

    def direct(i):
        r = pl.ds(pl.multiple_of(i * 16, 16), 16)
        value, slope = gelu_parts(yb[r, :])
        grad = dhy[r, :]
        hh = h[r, :]
        e[r, :] = grad * value
        dyb[r, :] = (grad * hh * slope).astype(bf)
        apad[r, :] = a[r, :]
        hpad[pl.ds(pl.multiple_of(i * 16 + 8, 8), 16), :] = hh

    loop(TOK // 16, direct)
    apad[TOK : TOK + 8, :] = jnp.ones((8, CH), f32)
    hpad[0:8, :] = state_in[...]

    def adjoint(i, carry):
        prod_in, state = carry
        r0 = TOK - 8 - i * 8
        r = pl.ds(pl.multiple_of(r0, 8), 8)
        next_a = ahead(apad[pl.ds(pl.multiple_of(r0, 8), 16), :], 1)
        pa, qb = scan8(next_a, e[r, :], True)
        qb = qb + pa * state
        pa = pa * prod_in
        q[r, :] = qb
        prod[r, :] = pa
        return pa[0:1, :], qb[0:1, :]

    last = lax.fori_loop(
        0, TOK // 8, adjoint, (jnp.ones((1, CH), f32), jnp.zeros((1, CH), f32))
    )
    mine[...] = jnp.zeros((8, CH), f32)
    total[...] = jnp.zeros((8, CH), f32)
    mine[0:1, :] = total_a[0:1, :]
    mine[1:2, :] = a[0:1, :] * last[1]
    came = line_prefix(mine, quad, rows, total, send, recv, 0, True)

    def point(i, carry):
        s_rate, s_input, s_decay = carry
        r = pl.ds(pl.multiple_of(i * 8, 8), 8)
        qq = q[r, :] + prod[r, :] * came
        aa, rr, gg, mm, cc = a[r, :], rate[r, :], gin[r, :], m[r, :], c[r, :]
        earlier = pltpu.roll(hpad[pl.ds(pl.multiple_of(i * 8, 8), 16), :], 1, 0)[8:16, :]
        grad_log = aa * (qq * earlier - qq * gg * cc * aa / mm)
        pr = -8.0 * vec[7:8, :] * grad_log * rr * (1.0 - rr)
        pi = qq * mm * cc * gg * (1.0 - gg)
        pri[r, 0:CH] = pr
        pri[r, CH:] = pi
        dc[r, :] = qq * mm * gg
        return s_rate + pr, s_input + pi, s_decay + 8.0 * rr * vec[8:9, :] * grad_log

    none = jnp.zeros((8, CH), f32)
    s_rate, s_input, s_decay = lax.fori_loop(0, TOK // 8, point, (none, none, none))

    def spread(i):
        r = pl.ds(pl.multiple_of(i * 128, 128), 128)
        dc[r, :] = dc[r, :] + dot3(split(pri[r, :]), (gate_hi[...], gate_lo[...]), ((1,), (1,)))

    loop(TOK // 128, spread)
    edge = pltpu.make_async_remote_copy(
        src_ref=dc.at[pl.ds(0, 8), :],
        dst_ref=halo,
        send_sem=send.at[10],
        recv_sem=recv.at[10],
        device_id=plane_device(before),
        device_id_type=MESH,
    )
    edge.start()
    dgate[...] = dot3(split(c[...]), split(pri[...]), ((0,), (0,)))
    edge.wait_recv()
    dc[TOK : TOK + 8, :] = jnp.where(block < 31, halo[...], 0.0)

    def taps(i, carry):
        r = i * 16
        here = pl.ds(pl.multiple_of(r, 16), 16)
        later = dc[pl.ds(pl.multiple_of(r, 16), 24), :]
        near = ext[pl.ds(pl.multiple_of(r, 16), 24), :]
        dd = later[0:16, :]
        out = vec[0:1, :] * dd
        for k in (1, 2, 3):
            out = out + vec[k : k + 1, :] * ahead(later, k)
        dxb[here, :] = out.astype(bf)

        def fold(v):
            return v[0:8, :] + v[8:16, :]

        got = [carry[0] + fold(dd)]
        for k in range(4):
            got.append(carry[1 + k] + fold(dd * behind(near, k)))
        return tuple(got)

    s_bias, *s_taps = lax.fori_loop(0, TOK // 16, taps, (none,) * 5)

    def put(row, value):
        sums[row : row + 1, :] = jnp.sum(value, axis=0, keepdims=True)

    for k in range(4):
        put(k, s_taps[k])
    put(4, s_bias)
    put(5, s_rate)
    put(6, s_input)
    put(7, s_decay)
    edge.wait_send()


def backward_scan(dhy, yb, gate_hi, gate_lo, vec, c, rate, gin, a, m, h, ext, state_in, total_a):
    return pl.pallas_call(
        backward_kernel,
        out_shape=(
            shape((TOK, CH), bf),
            shape((TOK, CH), bf),
            shape((CH, 2 * CH), f32),
            shape((8, CH), f32),
        ),
        in_specs=[VMEM] * 14,
        out_specs=[VMEM] * 4,
        scratch_shapes=[
            pltpu.VMEM((TOK, CH), f32),
            pltpu.VMEM((TOK + 8, CH), f32),
            pltpu.VMEM((TOK + 8, CH), f32),
            pltpu.VMEM((TOK, CH), f32),
            pltpu.VMEM((TOK, CH), f32),
            pltpu.VMEM((TOK, 2 * CH), f32),
            pltpu.VMEM((TOK + 8, CH), f32),
            pltpu.VMEM((8, CH), f32),
            pltpu.VMEM((8, CH), f32),
            pltpu.VMEM((4, 8, CH), f32),
            pltpu.VMEM((8, 8, CH), f32),
            pltpu.VMEM((8, CH), f32),
            pltpu.SemaphoreType.DMA((11,)),
            pltpu.SemaphoreType.DMA((11,)),
        ],
        compiler_params=params(5),
        name="backward_scan",
    )(dhy, yb, gate_hi, gate_lo, vec, c, rate, gin, a, m, h, ext, state_in, total_a)


def dot(p, q):
    return jnp.dot(p, q, preferred_element_type=f32)


def dot_t0(p, q):
    return lax.dot_general(p, q, (((0,), (0,)), ((), ())), preferred_element_type=f32)


def dot_t1(p, q):
    return lax.dot_general(p, q, (((1,), (1,)), ((), ())), preferred_element_type=f32)


def place():
    ylo, x, yhi, core = (lax.axis_index(n) for n in ("ylo", "x", "yhi", "core"))
    return ylo, x, yhi, core

def x_device(i):
    return {"x": i}

def y_device(i):
    return {"yhi": i // 2, "ylo": lax.rem(i, 2)}

def around(i):
    return lax.rem(i + 1, 4), lax.rem(i + 3, 4), lax.rem(i + 2, 4)

def plane_neighbours():
    ylo, x, yhi, core = place()
    y = yhi * 2 + ylo
    xr, xl, _ = around(x)
    yr, yl, _ = around(y)
    return [x_device(xr), x_device(xl), y_device(yr), y_device(yl), {"core": 1 - core}]

class Sender:
    def __init__(self, send, recv, base):
        self.send, self.recv, self.next, self.all = send, recv, base, []
    def __call__(self, source, target, device):
        copy = pltpu.make_async_remote_copy(
            src_ref=source, dst_ref=target, send_sem=self.send.at[self.next], recv_sem=self.recv.at[self.next],
            device_id=device, device_id_type=MESH)
        copy.start()
        self.next += 1
        self.all.append(copy)
        return copy
    def drain(self):
        for copy in self.all:
            copy.wait_send()

def got(copies):
    for copy in copies:
        copy.wait_recv()

GATHER_COPIES = 32
def cut(r):
    a = (r // 32) * 16
    a1 = ((a // 16 + 1) // 2) * 16
    b1 = (((r - a) // 16 + 1) // 2) * 16
    return a, a1, b1

def plane_gather(own, full, send, recv, base, local):
    put = Sender(send, recv, base)
    k, r, _ = own.shape
    ylo, x, yhi, core = place()
    y = yhi * 2 + ylo
    xr, xl, xf = around(x)
    yr, yl, yf = around(y)
    a, a1, b1 = cut(r)
    top, bottom = pl.ds(0, a), pl.ds(a, r - a)
    top1, top2 = pl.ds(0, a1), pl.ds(a1, a - a1)
    bot1, bot2 = pl.ds(a, b1), pl.ds(a + b1, r - a - b1)
    sib = {"core": 1 - core}
    def cols(lo, xx):
        return pl.ds(pl.multiple_of(lo * 1024 + xx * 256, 256), 256)
    def one(rows, yy, xx):
        return full.at[:, (yy // 2) * 2 + core, rows, cols(lax.rem(yy, 2), xx)]
    def row(rows, yy):
        return full.at[:, (yy // 2) * 2 + core, rows, pl.ds(pl.multiple_of(lax.rem(yy, 2) * 1024, 1024), 1024)]
    keep = pltpu.make_async_copy(own, one(pl.ds(0, r), y, x), local)
    keep.start()
    ha, hb = own.at[:, top, :], own.at[:, bottom, :]
    p = [put(ha, one(top, y, x), x_device(xr)), put(ha, one(top, y, x), x_device(xl)),
         put(hb, one(bottom, y, x), y_device(yr)), put(hb, one(bottom, y, x), y_device(yl))]
    yield
    got(p)
    keep.wait()
    p = [put(one(top1, y, xl), one(top1, y, xl), x_device(xr)), put(one(top2, y, xr), one(top2, y, xr), x_device(xl)),
         put(one(bot1, yl, x), one(bot1, yl, x), y_device(yr)), put(one(bot2, yr, x), one(bot2, yr, x), y_device(yl))]
    yield
    got(p)
    def pieces(rows, xx):
        out = []
        for lo in (0, 1):
            for hi in (0, 1):
                out.append(full.at[:, 2 * hi + core, rows, cols(lo, xx)])
        return out
    def send_row(rows, yy, device):
        return [put(row(rows, yy), row(rows, yy), device)]
    def send_col(rows, xx, device):
        return [put(s, s, device) for s in pieces(rows, xx)]
    p = send_row(top, y, y_device(yr)) + send_row(top, y, y_device(yl))
    p += send_col(bottom, x, x_device(xr)) + send_col(bottom, x, x_device(xl))
    s = send_row(top, y, sib) + send_col(bottom, x, sib)
    yield
    got(p)
    p = send_row(top1, yl, y_device(yr)) + send_row(top2, yr, y_device(yl))
    p += send_col(bot1, xl, x_device(xr)) + send_col(bot2, xr, x_device(xl))
    s += send_row(top, yl, sib) + send_row(top, yr, sib) + send_col(bottom, xl, sib) + send_col(bottom, xr, sib)
    yield
    got(p)
    s += send_row(top, yf, sib) + send_col(bottom, xf, sib)
    yield
    got(s)
    put.drain()
    assert put.next - base <= 56, put.next - base


def run_all(steps):
    for _ in steps:
        pass


def weights_kernel(own, full, send, recv, local):
    meet(plane_neighbours())
    run_all(plane_gather(own, full, send, recv, 0, local))


def gather_weights(own, cid):
    k, r, _ = own.shape
    return pl.pallas_call(
        weights_kernel,
        out_shape=shape((k, 4, r, D), bf),
        in_specs=[pl.BlockSpec(memory_space=pl.ANY)],
        out_specs=pl.BlockSpec(memory_space=pl.ANY),
        scratch_shapes=[
            pltpu.SemaphoreType.DMA((56,)),
            pltpu.SemaphoreType.DMA((56,)),
            pltpu.SemaphoreType.DMA,
        ],
        compiler_params=params(cid),
        name="gather_weights",
    )(own)


def plane_sum(part, out, fold, ga, gb, ha, hb, sa, sb, ra2, rb2, send, recv, base):
    put = Sender(send, recv, base)
    _, r, _ = part.shape
    ylo, x, yhi, core = place()
    y = yhi * 2 + ylo
    xr, xl, xf = around(x)
    yr, yl, yf = around(y)
    a = -(-r // 64) * 32
    h, g = a // 2, (r - a) // 2
    sib = {"core": 1 - core}
    p = []
    for hi in (0, 1):
        p.append(put(part.at[2 * hi + 1 - core], fold.at[hi], sib))
    yield
    for hi in (0, 1):
        p[hi].wait_recv()
        def body(i, carry, hi=hi):
            rr = pl.ds(pl.multiple_of(i * 16, 16), 16)
            fold[hi, rr, :] = (fold[hi, rr, :].astype(f32) + part[2 * hi + core, rr, :].astype(f32)).astype(bf)
            return carry
        lax.fori_loop(0, r // 16, body, 0)
    def ycols(yy):
        return pl.ds(pl.multiple_of(lax.rem(yy, 2) * 1024, 1024), 1024)
    def a_block(yy, first):
        return fold.at[yy // 2, pl.ds(0 if first else h, h), ycols(yy)]
    def b_block(xx, first, l):
        return fold.at[:, pl.ds(a + (0 if first else g), g), pl.ds(pl.multiple_of(l * 1024 + xx * 256, 256), 256)]
    yR, yL, xR, xL = y_device(yr), y_device(yl), x_device(xr), x_device(xl)
    def sendb(i, xx, first, dev):
        return [put(b_block(xx, first, l), gb.at[i, l], dev) for l in (0, 1)]
    pa = [put(a_block(yf, True), ga.at[0], yR), put(a_block(yf, False), ga.at[1], yL)]
    pb = [sendb(0, xf, True, xR), sendb(1, xf, False, xL)]
    pa += [put(a_block(yr, False), ga.at[2], yR), put(a_block(yl, True), ga.at[3], yL)]
    pb += [sendb(2, xr, False, xR), sendb(3, xl, True, xL)]
    yield
    def add_a(dst, i, block, n):
        def body(j, carry):
            rr = pl.ds(pl.multiple_of(j * 16, 16), 16)
            dst[rr, :] = (ga[i, rr, :].astype(f32) + block[rr, :].astype(f32)).astype(bf)
            return carry
        lax.fori_loop(0, n // 16, body, 0)
    def add_b(dst, i, xx, first):
        for l in (0, 1):
            for hi in (0, 1):
                block = fold.at[hi, pl.ds(a + (0 if first else g), g), pl.ds(pl.multiple_of(l * 1024 + xx * 256, 256), 256)]
                def body(j, carry):
                    rr = pl.ds(pl.multiple_of(j * 16, 16), 16)
                    dst[l, hi, rr, :] = (gb[i, l, hi, rr, :].astype(f32) + block[rr, :].astype(f32)).astype(bf)
                    return carry
                lax.fori_loop(0, g // 16, body, 0)
    pa[0].wait_recv()
    add_a(sa.at[0], 0, a_block(yr, True), h)
    pa.append(put(sa.at[0], ga.at[4], yR))
    got(pb[0])
    add_b(sb.at[0], 0, xr, True)
    pb.append([put(sb.at[0], gb.at[4], xR)])
    pa[1].wait_recv()
    add_a(sa.at[1], 1, a_block(yl, False), h)
    pa.append(put(sa.at[1], ga.at[5], yL))
    got(pb[1])
    add_b(sb.at[1], 1, xl, False)
    pb.append([put(sb.at[1], gb.at[5], xL)])
    yield
    def fin_a(first, i, j):
        def body(n, carry):
            rr = pl.ds(pl.multiple_of(n * 16, 16), 16)
            block = a_block(y, first)
            ra2[pl.ds(pl.multiple_of((0 if first else h) + n * 16, 16), 16), :] = (
                block[rr, :].astype(f32) + ga[i, rr, :].astype(f32) + ga[j, rr, :].astype(f32)).astype(bf)
            return carry
        lax.fori_loop(0, h // 16, body, 0)
    def fin_b(first, i, j):
        for l in (0, 1):
            for hi in (0, 1):
                block = fold.at[hi, pl.ds(a + (0 if first else g), g), pl.ds(pl.multiple_of(l * 1024 + x * 256, 256), 256)]
                def body(n, carry):
                    rr = pl.ds(pl.multiple_of(n * 16, 16), 16)
                    rb2[l, hi, pl.ds(pl.multiple_of((0 if first else g) + n * 16, 16), 16), :] = (
                        block[rr, :].astype(f32) + gb[i, l, hi, rr, :].astype(f32) + gb[j, l, hi, rr, :].astype(f32)).astype(bf)
                    return carry
                lax.fori_loop(0, g // 16, body, 0)
    got([pa[3], pa[4]])
    fin_a(True, 3, 4)
    got([pa[2], pa[5]])
    fin_a(False, 2, 5)
    got(pb[3] + pb[4])
    fin_b(True, 3, 4)
    got(pb[2] + pb[5])
    fin_b(False, 2, 5)
    def a2(xx, first):
        return ra2.at[pl.ds(0 if first else h, h), pl.ds(pl.multiple_of(xx * 256, 256), 256)]
    def b2(yy, first):
        return rb2.at[lax.rem(yy, 2), yy // 2, pl.ds(0 if first else g, g), :]
    qa = [put(a2(xf, True), ha.at[0], xR), put(a2(xf, False), ha.at[1], xL), put(a2(xr, False), ha.at[2], xR), put(a2(xl, True), ha.at[3], xL)]
    qb = [put(b2(yf, True), hb.at[0], yR), put(b2(yf, False), hb.at[1], yL), put(b2(yr, False), hb.at[2], yR), put(b2(yl, True), hb.at[3], yL)]
    yield
    sa2, sb2 = ha.at[pl.ds(6, 2)], hb.at[pl.ds(6, 2)]
    qa[0].wait_recv()
    sa2[0] = (ha[0].astype(f32) + a2(xr, True)[...].astype(f32)).astype(bf)
    qa.append(put(sa2.at[0], ha.at[4], xR))
    qb[0].wait_recv()
    sb2[0] = (hb[0].astype(f32) + b2(yr, True)[...].astype(f32)).astype(bf)
    qb.append(put(sb2.at[0], hb.at[4], yR))
    qa[1].wait_recv()
    sa2[1] = (ha[1].astype(f32) + a2(xl, False)[...].astype(f32)).astype(bf)
    qa.append(put(sa2.at[1], ha.at[5], xL))
    qb[1].wait_recv()
    sb2[1] = (hb[1].astype(f32) + b2(yl, False)[...].astype(f32)).astype(bf)
    qb.append(put(sb2.at[1], hb.at[5], yL))
    yield
    got(qa[2:] + qb[2:])
    def w(v): return v.astype(f32)
    out[0:h, :] = w(a2(x, True)[...]) + w(ha[3]) + w(ha[4])
    out[h:a, :] = w(a2(x, False)[...]) + w(ha[2]) + w(ha[5])
    out[a:a + g, :] = w(b2(y, True)[...]) + w(hb[3]) + w(hb[4])
    out[a + g:, :] = w(b2(y, False)[...]) + w(hb[2]) + w(hb[5])
    put.drain()


def sum_scratch(r):
    a = -(-r // 64) * 32
    h, g = a // 2, (r - a) // 2
    V = pltpu.VMEM
    return [V((2, r, 2048), bf), V((6, h, 1024), bf), V((6, 2, 2, g, 256), bf), V((8, h, 256), bf), V((8, g, 256), bf),
            V((2, h, 1024), bf), V((2, 2, 2, g, 256), bf), V((a, 1024), bf), V((2, 2, r - a, 256), bf)]


def grads_kernel(part, out, *rest):
    meet(plane_neighbours())
    run_all(plane_sum(part, out, *rest, 0))


def sum_grads(part, cid):
    _, r, _ = part.shape
    return pl.pallas_call(
        grads_kernel,
        out_shape=shape((r, 256), f32),
        in_specs=[VMEM],
        out_specs=VMEM,
        scratch_shapes=sum_scratch(r)
        + [pltpu.SemaphoreType.DMA((30,)), pltpu.SemaphoreType.DMA((30,))],
        compiler_params=params(cid),
        name="sum_grads",
    )(part)


def small_kernel(blocks, gains, small, gain, zgot, qgot, qgain, rgot, rgain, mine, send, recv):
    z = lax.axis_index("z")
    me = lax.axis_index("yhi") * 2 + lax.axis_index("core")
    row = lax.axis_index("ylo") * 4 + lax.axis_index("x")
    meet(line_devices() + z_others())
    put = Sender(send, recv, 0)
    zs, qs = [], []
    for j in (1, 2, 3):
        to = lax.rem(z + j, 4)
        zs.append(put(gains.at[to], zgot.at[j - 1], {"z": to}))
    for j in (1, 2, 3):
        to = lax.rem(me + j, 4)
        qs.append(put(blocks.at[to], qgot.at[j - 1], quad_device(to)))
    got(zs)
    qgain[3] = gains[z] + zgot[0] + zgot[1] + zgot[2]
    for j in (1, 2, 3):
        to = lax.rem(me + j, 4)
        qs.append(put(qgain.at[3, to], qgain.at[j - 1, 0], quad_device(to)))
    got(qs)
    mine[...] = blocks[me] + qgot[0] + qgot[1] + qgot[2]
    rgain[7] = qgain[3, me] + qgain[0, 0] + qgain[1, 0] + qgain[2, 0]
    rs = []

    def seq(j):
        to = lax.rem(row + j, 8)
        return to, {"ylo": to // 4, "x": lax.rem(to, 4)}

    for j in range(1, 8):
        to, device = seq(j)
        rs.append(put(mine.at[pl.ds(pl.multiple_of(to * 48, 8), 48), :], rgot.at[j - 1], device))
        rs.append(put(rgain.at[7], rgain.at[j - 1], device))
    got(rs)
    own = pl.ds(pl.multiple_of(row * 48, 8), 48)
    total = mine[own, :]
    gain_total = rgain[7]
    for j in range(7):
        total = total + rgot[j]
        gain_total = gain_total + rgain[j]
    small[own, :] = total
    gain[...] = gain_total
    ag = []
    for j in range(1, 8):
        _, device = seq(j)
        ag.append(put(small.at[own, :], small.at[own, :], device))
    got(ag)
    put.drain()


def small_sums(blocks, gains):
    return pl.pallas_call(
        small_kernel,
        out_shape=(shape((384, HW), f32), shape((8, 128), f32)),
        in_specs=[VMEM] * 2,
        out_specs=[VMEM] * 2,
        scratch_shapes=[
            pltpu.VMEM((3, 4, 8, 128), f32),
            pltpu.VMEM((3, 384, HW), f32),
            pltpu.VMEM((4, 4, 8, 128), f32),
            pltpu.VMEM((7, 48, HW), f32),
            pltpu.VMEM((8, 8, 128), f32),
            pltpu.VMEM((384, HW), f32),
            pltpu.SemaphoreType.DMA((30,)),
            pltpu.SemaphoreType.DMA((30,)),
        ],
        compiler_params=params(8),
        name="small_sums",
    )(blocks, gains)


def to_tokens(own):
    return lax.all_to_all(own, QUAD, split_axis=1, concat_axis=0, tiled=True)


def block_diagonal(blocks):
    rows = [
        jnp.concatenate(
            [jnp.zeros((HW, HW * i), f32), blocks[i], jnp.zeros((HW, HW * (3 - i)), f32)], axis=1
        )
        for i in range(4)
    ]
    return jnp.concatenate(rows, axis=0)


def per_device(
    block_in, cotangent, norm_one, rec_in, rec_gate, conv_weight, conv_bias,
    rate_weight, rate_bias, input_weight, input_bias, decay_code, rec_out,
    norm_two, mlp_gate, mlp_up, mlp_down,
):
    decay = decay_code.astype(f32) / 256.0
    vectors = jnp.concatenate(
        [
            conv_weight,
            conv_bias[None],
            rate_bias[None],
            input_bias[None],
            jax.nn.softplus(-decay)[None],
            jax.nn.sigmoid(-decay)[None],
            jnp.zeros((7, HW), f32),
        ],
        axis=0,
    )
    norms = jnp.concatenate([norm_one[None], norm_two[None], jnp.zeros((6, 128), f32)], axis=0)
    x_full, rate_all, input_all, vec_all, norms_all = entry(
        block_in, rate_weight[0], input_weight[0], vectors, norms
    )
    w_rec = gather_weights(jnp.stack([rec_in.T, rec_gate.T, rec_out]), 6).reshape(3, CH, D)
    w_mlp = gather_weights(jnp.stack([mlp_gate.T, mlp_up.T, mlp_down]), 7).reshape(3, 1536, D)
    w_in, w_gate_rec, w_out = w_rec[0], w_rec[1], w_rec[2]
    w_gate, w_up, w_down = w_mlp[0], w_mlp[1], w_mlp[2]
    vec = vec_all.transpose(1, 0, 2).reshape(16, CH)
    gains = norms_all.reshape(16, 8, 128)
    gain_one = gains[:, 0].reshape(1, D)
    gain_two = gains[:, 1].reshape(1, D)
    gate_hi, gate_lo = split(
        jnp.concatenate([block_diagonal(rate_all), block_diagonal(input_all)], axis=1)
    )

    x_rows = x_full.astype(f32)
    inv_one = lax.rsqrt(jnp.mean(x_rows * x_rows, axis=1, keepdims=True) + EPS)
    n_one = (x_rows * inv_one * gain_one).astype(bf)
    xb = dot_t1(n_one, w_in)
    yb = dot_t1(n_one, w_gate_rec)
    c, rate, gin, a, m, h, hy, ext, state_in, total_a = forward_scan(
        xb.astype(bf), yb, gate_hi, gate_lo, vec
    )
    mix_full, mix_own = allsum(dot(hy, w_out).astype(bf))
    z = lax.axis_index("z")
    x_own = lax.dynamic_slice(x_full, (0, z * 512), (TOK, 512)).astype(f32)
    z_rows = x_rows + mix_full.astype(f32)
    z_own = x_own + mix_own
    inv_two = lax.rsqrt(jnp.mean(z_rows * z_rows, axis=1, keepdims=True) + EPS)
    n_two = (z_rows * inv_two * gain_two).astype(bf)

    g = dot_t1(n_two, w_gate)
    u = dot_t1(n_two, w_up)
    gelu_g, slope_g = gelu_parts(g)
    act = (gelu_g * u).astype(bf)
    cot_full = gather_tokens(cotangent)
    dact = dot_t1(cot_full, w_down)
    dg = (dact * u * slope_g).astype(bf)
    du = (dact * gelu_g).astype(bf)
    inner_two = jnp.sum(dg.astype(f32) * g + du.astype(f32) * u, axis=1, keepdims=True)
    dn_two = dot(dg, w_gate) + dot(du, w_up)
    step_two = dn_two * inv_two * gain_two - z_rows * (inv_two * inv_two * inner_two / D)
    gain_two_sums = jnp.sum(dn_two * z_rows * inv_two, axis=0)
    back_full, back_own = allsum(step_two.astype(bf))
    dmix = (cot_full.astype(f32) + back_full.astype(f32)).astype(bf)
    cot_own = lax.dynamic_slice(cot_full, (0, z * 512), (TOK, 512)).astype(f32)
    dz_own = cot_own + back_own

    mlp_own = ownsum(dot(act, w_down).astype(bf))
    block_out = to_tokens((z_own + mlp_own).astype(bf))
    grad_down = sum_grads(dot_t0(act, cot_full).astype(bf).reshape(4, 384, D), 9)
    grad_gate = sum_grads(dot_t0(dg, n_two).astype(bf).reshape(4, 384, D), 9).T
    grad_up = sum_grads(dot_t0(du, n_two).astype(bf).reshape(4, 384, D), 9).T

    dhy = dot_t1(dmix, w_out)
    dxb, dyb, dgate, sums = backward_scan(
        dhy, yb, gate_hi, gate_lo, vec, c, rate, gin, a, m, h, ext, state_in, total_a
    )
    inner_one = jnp.sum(dxb.astype(f32) * xb + dyb.astype(f32) * yb, axis=1, keepdims=True)
    dn_one = dot(dxb, w_in) + dot(dyb, w_gate_rec)
    step_one = dn_one * inv_one * gain_one - x_rows * (inv_one * inv_one * inner_one / D)
    gain_one_sums = jnp.sum(dn_one * x_rows * inv_one, axis=0)
    grad_own = dz_own + ownsum(step_one.astype(bf))
    grad_in = to_tokens(grad_own.astype(bf)).astype(f32)
    grad_rec = jnp.concatenate(
        [dot_t0(p, q).astype(bf).reshape(4, HW, D) for p, q in ((dxb, n_one), (dyb, n_one), (hy, dmix))],
        axis=1,
    )
    grad_rec = sum_grads(grad_rec, 10)
    grad_rec_in, grad_rec_gate, grad_out = grad_rec[:HW].T, grad_rec[HW : 2 * HW].T, grad_rec[2 * HW :]

    blocks = [
        jnp.concatenate(
            [
                dgate[HW * i : HW * (i + 1), HW * i : HW * (i + 1)],
                dgate[HW * i : HW * (i + 1), CH + HW * i : CH + HW * (i + 1)],
                sums[:, HW * i : HW * (i + 1)],
                jnp.zeros((56, HW), f32),
            ],
            axis=0,
        )
        for i in range(4)
    ]
    gains = jnp.stack([gain_one_sums.reshape(4, 4, 128), gain_two_sums.reshape(4, 4, 128)], axis=2)
    gains = jnp.concatenate([gains, jnp.zeros((4, 4, 6, 128), f32)], axis=2)
    small, gain_sums = small_sums(jnp.stack(blocks), gains)
    vector_grads = small[2 * HW : 2 * HW + 8]
    return (
        block_out,
        grad_in,
        gain_sums[0],
        grad_rec_in,
        grad_rec_gate,
        vector_grads[0:4],
        vector_grads[4],
        small[:HW][None],
        vector_grads[5],
        small[HW : 2 * HW][None],
        vector_grads[6],
        vector_grads[7],
        grad_out,
        gain_sums[1],
        grad_gate,
        grad_up,
        grad_down,
    )


def solution(mesh):
    fine = Mesh(mesh.devices.reshape(2, 4, 4, 2, 2), ("ylo", "x", "z", "yhi", "core"))
    both = P(SEQ, HEAD)
    swap = P(HEAD, SEQ)
    vector = P(HEAD)
    stack = P(HEAD, None, None)
    taps = P(None, HEAD)
    return jax.shard_map(
        per_device,
        mesh=fine,
        in_specs=(
            both, both, vector, both, both, taps, vector, stack, vector, stack, vector, vector,
            swap, vector, both, both, swap,
        ),
        out_specs=(
            both, both, vector, both, both, taps, vector, stack, vector, stack, vector, vector,
            swap, vector, both, both, swap,
        ),
        check_vma=False,
    )
```

time: 2590 us -> 758 us (0.29)
  local copies, waits for them, and re-layouts: 1110 us -> 45.8 us
  waiting for transfers between devices: 853 us -> 8.26 us
  Pallas kernels: 0 us -> 560 us
  blocking collectives: 287 us -> 0 us
  other arithmetic: 125 us -> 34.6 us
  matrix products: 177 us -> 91.7 us
    slice x140 -> x8, local copies, waits for them, and re-layouts: 632 us -> 26.6 us  [the longest x1 15 us: per_device(): w_gate, w_up, w_down = (w_mlp[0], w_mlp[1], w_mlp[2])]
    reduce_scatter x10 -> x0, waiting for transfers between devices: 569 us -> none  [the longest x2 294 us: feature_sum(): lax.psum_scatter(partial_rows, 'head', scatter_dimension=1, tiled=True)]
    pallas_call x0 -> x15, Pallas kernels: none -> 560 us  [the longest x4 144 us: sum_grads(): pl.pallas_call(grads_kernel, out_shape=shape((r, 256), f32), in_specs=[VM...]
    pad x80 -> x0, local copies, waits for them, and re-layouts: 395 us -> none  [the longest x40 209 us: per_device(): lax.associative_scan(pair_combine, (next_decay, grad_direct), reverse=Tru...]
    all_gather x7 -> x0, waiting for transfers between devices: 206 us -> none  [the longest x2 81 us: grads_gather(): lax.all_gather(grad_rows.astype(jnp.bfloat16), 'head', axis=1, tiled=True)]
    all_gather x6 -> x0, blocking collectives: 146 us -> none  [the longest x3 53.3 us: prefix(): gathered = jax.tree.map(lambda a: lax.all_gather(a, axis), part)]
    psum x4 -> x0, blocking collectives: 141 us -> none  [the longest x2 73.6 us: norm_forward(): summed = lax.psum(jnp.sum(values * values, axis=1), 'head')]
    dot_general x24 -> x18, matrix products: 177 us -> 91.7 us  [the longest x6 32.9 us: dot_t1(): lax.dot_general(p, q, (((1,), (1,)), ((), ())), preferred_element_type=f32)]
  transfers between devices with their start and end apart: 20 -> 2, of which waited for: 12 -> 1; matrix products, arithmetic and copies ran while one was open for 32% -> 10% of each run, Pallas kernels for 0% -> 38%
where the time goes in v1:
time: 758 us; the launch traced here: 749 us
  Pallas kernels  560 us (74%)
  matrix products  91.7 us (12%)
  local copies, waits for them, and re-layouts  45.8 us (6%)
  other arithmetic  34.6 us (5%)
  waiting for transfers between devices  8.26 us (1%)
  starting transfers between devices  7.62 us (1%)
    pallas_call x4, Pallas kernels, sum_grads(): pl.pallas_call(grads_kernel, out_shape=shape((r, 256), f32), in_specs=[VM...  144 us
    pallas_call x2, Pallas kernels, gather_weights(): pl.pallas_call(weights_kernel, out_shape=shape((k, 4, r, D), bf), in_spec...  111 us
    pallas_call x2, Pallas kernels, allsum(): pl.pallas_call(allsum_kernel, out_shape=(shape((TOK, D), bf), shape((TOK,...  84.6 us
    pallas_call x2, Pallas kernels, ownsum(): pl.pallas_call(sum_kernel, out_shape=shape((TOK, 512), f32), in_specs=[VM...  46.5 us
    pallas_call x1, Pallas kernels, small_sums(): pl.pallas_call(small_kernel, out_shape=(shape((384, HW), f32), shape((8,...  40.4 us
    pallas_call x1, Pallas kernels, entry(): pl.pallas_call(entry_kernel, out_shape=(shape((TOK, D), bf), shape((4, HW...  37.5 us
    pallas_call x1, Pallas kernels, backward_scan(): pl.pallas_call(backward_kernel, out_shape=(shape((TOK, CH), bf), shape((T...  35.2 us
    dot_general x6, matrix products, dot_t1(): lax.dot_general(p, q, (((1,), (1,)), ((), ())), preferred_element_type=f32)  32.9 us
  transfers between devices with their start and end apart: 2, of which 1 were waited for; matrix products, arithmetic and copies ran while one was open for 10% of the time, Pallas kernels for 38%

profile of v1, /device:TPU:0, one launch (start us, length us, event | category | flops | bytes accessed | tf_op | source)
XLA Modules:
  0.0 749.3 jit_solution(9112974054991747213)
XLA Ops:
  1.5 1.3 maximum_maximum_fusion.1.norms
  2.9 1.9 concatenate.57.vectors
  4.8 37.5 %entry.1 = (bf16[512,2048]{1,0:T(8,128)(2,1)}, f32[4,160,160]{2,1,0:T(8,128)}, f32[4,160,160]{2,1,0:T(8,128)}, f32[4,16,160]{2,1,0:T(8,128)}, f32[4,4,8,128]{3,2,1,0:T(8,128)}) custom-call(bf16[2048,128]{1,0:T(8,128)(2,1)} %tokens.2, f32[160,160]{1,0:T(8,128)} %bitcast.159, f32[160,160]{1,0:T(8,128)} %bitcast.160, f32[16,160]{1,0:T(8,128)} %concatenate.57.vectors, ...), custom_call_target="tpu_custom_call" | custom-call | tf_op jit(solution)/shard_map/entry/pallas_call | solution.py:217
  42.4 2.1 fusion
  44.4 0.9 fusion.35
  46.1 39.0 %gather_weights.2 = bf16[3,4,160,2048]{3,2,1,0:T(8,128)(2,1)} custom-call(bf16[3,160,256]{2,1,0:T(8,128)(2,1)} %pad_maximum_fusion.3.own), custom_call_target="tpu_custom_call" | custom-call | tf_op jit(solution)/shard_map/gather_weights/pallas_call | solution.py:817
  85.2 5.0 fusion.31
  90.2 2.9 fusion.25.yb
  93.1 2.7 fusion.37
  96.6 1.5 slice_bitcast_fusion.6
  98.1 10.5 %subtract_convert_fusion.1 = (bf16[640,1280]{1,0:T(8,128)(2,1)}, bf16[640,1280]{1,0:T(8,128)(2,1)}) fusion(f32[160,160]{1,0:T(8,128)S(1)} %get-tuple-element.129, f32[160,160]{1,0:T(8,128)S(1)} %broadcast.77, f32[160,160]{1,0:T(8,128)S(1)} %get-tuple-element.130, f32[160,320]{1,0:T(8,128)S(1)} %broadcast.78, f32[160,160]{1,0:T(8,128)S(1)} %get-tuple-element.128, ...), kind=kLoop, calls=%fused_computation.37 | loop fusion | flops 28672000 | bytes 4403200 | tf_op jit(solution)/shard_map/convert_element_type | solution.py:376
  108.7 29.6 %forward_scan.1 = (f32[512,640]{1,0:T(8,128)}, f32[512,640]{1,0:T(8,128)}, f32[512,640]{1,0:T(8,128)}, f32[512,640]{1,0:T(8,128)}, f32[512,640]{1,0:T(8,128)}, /...) custom-call(bf16[512,640]{1,0:T(8,128)(2,1)} %get-tuple-element.155., ...), custom_call_target="tpu_custom_call" | custom-call | tf_op jit(solution)/shard_map/forward_scan/pallas_call | solution.py:519
  138.3 4.2 convolution_convert_fusion.7.part
  142.5 41.2 %allsum.2 = (bf16[512,2048]{1,0:T(8,128)(2,1)}, f32[512,512]{1,0:T(8,128)}) custom-call(bf16[512,2048]{1,0:T(8,128)(2,1)} %convolution_convert_fusion.7.part), custom_call_target="tpu_custom_call" | custom-call | tf_op jit(solution)/shard_map/allsum/pallas_call | solution.py:265
  183.7 2.3 multiply_reduce_fusion.1
  186.0 1.7 copy.43
  187.8 1.7 copy.44
  189.5 2.0 pad_maximum_fusion.2.own
  191.5 72.3 %gather_weights.3 = bf16[3,4,384,2048]{3,2,1,0:T(8,128)(2,1)} custom-call(bf16[3,384,256]{2,1,0:T(8,128)(2,1)} %pad_maximum_fusion.2.own), custom_call_target="tpu_custom_call" | custom-call | tf_op jit(solution)/shard_map/gather_weights/pallas_call | solution.py:817
  263.8 15.0 %fusion.30 = (bf16[1,4,384,2048]{3,2,1,0:T(8,128)(2,1)}, bf16[1,4,384,2048]{3,2,1,0:T(8,128)(2,1)}, bf16[1,4,384,2048]{3,2,1,0:T(8,128)(2,1)}) fusion(bf16[3,4,384,2048]{3,2,1,0:T(8,128)(2,1)} %gather_weights.3), kind=kLoop, calls=%fused_computation.96 | loop fusion | bytes 37748736 | tf_op jit(solution)/shard_map/slice | solution.py:1086
  278.8 30.0 %gather_tokens.1 = bf16[512,2048]{1,0:T(8,128)(2,1)} custom-call(bf16[2048,128]{1,0:T(8,128)(2,1)} %tokens.3), custom_call_target="tpu_custom_call" | custom-call | tf_op jit(solution)/shard_map/gather_tokens/pallas_call | solution.py:245
  308.8 2.8 multiply_convert_fusion
  312.2 3.5 fusion.38
  315.7 3.5 convolution_bitcast_fusion
  319.3 17.4 %add_reduce_fusion = (f32[512]{0:T(512)S(1)}, bf16[512,1536]{1,0:T(8,128)(2,1)}, bf16[512,1536]{1,0:T(8,128)(2,1)}, bf16[512,1536]{1,0:T(8,128)(2,1)S(1)}) fusion(f32[512,1536]{1,0:T(8,128)S(1)} %fusion.38, f32[512,1536]{1,0:T(8,128)S(1)} %convolution_bitcast_fusion, bf16[512,2048]{1,0:T(8,128)(2,1)S(1)} %multiply_convert_fusion, ...), kind=kOutput, calls=%fused_computation.48 | convolution fusion | flops 3238526464 | bytes 19400704 | tf_op jit(solution)/shard_map/dot_general | solution.py:699
  336.7 1.2 copy-done.32
  337.9 4.6 convolution_convert_fusion.6.part
  342.5 24.2 %ownsum.2 = f32[512,512]{1,0:T(8,128)} custom-call(bf16[512,2048]{1,0:T(8,128)(2,1)} %convolution_convert_fusion.6.part), custom_call_target="tpu_custom_call" | custom-call | tf_op jit(solution)/shard_map/ownsum/pallas_call | solution.py:287
  366.7 2.5 copy_bitcast_fusion.1
  369.2 4.1 all-to-all-start
  373.4 6.1 fusion.39
  379.6 8.8 %subtract_convert_fusion = (bf16[512,2048]{1,0:T(8,128)(2,1)}, f32[512,2048]{1,0:T(8,128)}) fusion(bf16[512,2048]{1,0:T(8,128)(2,1)S(1)} %copy-done.2, bf16[512,2048]{1,0:T(8,128)(2,1)S(1)} %copy-done, f32[512]{0:T(512)S(1)} %multiply_multiply_fusion.2, f32[2048]{0:T(1024)S(1)} %bitcast.166, f32[512]{0:T(512)S(1)} %add_rsqrt_fusion, ...), kind=kOutput, calls=%fused_computation.19 | convolution fusion | flops 3230662656 | bytes 22556672 | tf_op jit(solution)/shard_map/dot_general | solution.py:691
  388.4 43.5 %allsum.3 = (bf16[512,2048]{1,0:T(8,128)(2,1)}, f32[512,512]{1,0:T(8,128)}) custom-call(bf16[512,2048]{1,0:T(8,128)(2,1)} %get-tuple-element.157.part), custom_call_target="tpu_custom_call" | custom-call | tf_op jit(solution)/shard_map/allsum/pallas_call | solution.py:265
  431.9 5.1 convolution_convert_fusion.3
  437.0 2.9 fusion.20.dhy
  439.9 5.4 convolution_convert_fusion.2
  445.2 5.4 convolution_convert_fusion.1
  450.6 35.2 %backward_scan.1 = (bf16[512,640]{1,0:T(8,128)(2,1)}, bf16[512,640]{1,0:T(8,128)(2,1)}, f32[640,1280]{1,0:T(8,128)}, f32[8,640]{1,0:T(8,128)}) custom-call(f32[512,640]{1,0:T(8,128)} %fusion.20.dhy, f32[512,640]{1,0:T(8,128)} %fusion.25.yb, bf16[640,1280]{1,0:T(8,128)(2,1)} %get-tuple-element.107.gate_hi, bf16[640,1280]{1,0:T(8,128)(2,1)} %get-tuple-element.106.gate_lo, ...), custom_call_target="tpu_custom_call" | custom-call | tf_op jit(solution)/shard_map/backward_scan/pallas_call | solution.py:659
  485.8 4.4 convolution_convert_fusion.5
  490.2 1.8 fusion.40
  492.1 5.4 convolution_convert_fusion
  497.5 3.1 convolution_convert_fusion.4
  501.0 2.0 fusion.32
  503.3 4.5 fusion.6
  508.6 1.3 pad_maximum_fusion.1.blocks
  509.9 40.4 %small_sums.1 = (f32[384,160]{1,0:T(8,128)}, f32[8,128]{1,0:T(8,128)}) custom-call(f32[4,384,160]{2,1,0:T(8,128)} %pad_maximum_fusion.1.blocks, f32[4,4,8,128]{3,2,1,0:T(8,128)} %maximum_maximum_fusion.gains), custom_call_target="tpu_custom_call" | custom-call | tf_op jit(solution)/shard_map/small_sums/pallas_call | solution.py:1027
  550.3 1.7 slice_bitcast_fusion
  552.1 3.9 pad_maximum_fusion.part
  556.0 1.4 fusion.34
  557.4 1.3 slice.163
  558.7 40.4 %sum_grads.4 = f32[480,256]{1,0:T(8,128)} custom-call(bf16[4,480,2048]{2,1,0:T(8,128)(2,1)} %pad_maximum_fusion.part), custom_call_target="tpu_custom_call" | custom-call | tf_op jit(solution)/shard_map/sum_grads/pallas_call | solution.py:966
  599.1 35.3 %sum_grads.5 = f32[384,256]{1,0:T(8,128)} custom-call(bf16[4,384,2048]{2,1,0:T(8,128)(2,1)} %bitcast.142), custom_call_target="tpu_custom_call" | custom-call | tf_op jit(solution)/shard_map/sum_grads/pallas_call | solution.py:966
  634.4 1.9 copy.48
  636.3 33.7 %sum_grads.6 = f32[384,256]{1,0:T(8,128)} custom-call(bf16[4,384,2048]{2,1,0:T(8,128)(2,1)} %bitcast.141), custom_call_target="tpu_custom_call" | custom-call | tf_op jit(solution)/shard_map/sum_grads/pallas_call | solution.py:966
  670.0 1.9 copy.49
  671.9 22.3 %ownsum.3 = f32[512,512]{1,0:T(8,128)} custom-call(bf16[512,2048]{1,0:T(8,128)(2,1)} %get-tuple-element.114.part), custom_call_target="tpu_custom_call" | custom-call | tf_op jit(solution)/shard_map/ownsum/pallas_call | solution.py:287
  694.3 35.0 %sum_grads.7 = f32[384,256]{1,0:T(8,128)} custom-call(bf16[4,384,2048]{2,1,0:T(8,128)(2,1)} %bitcast.143), custom_call_target="tpu_custom_call" | custom-call | tf_op jit(solution)/shard_map/sum_grads/pallas_call | solution.py:966
  729.3 2.1 copy_bitcast_fusion
  731.4 3.5 all-to-all-start.1
  734.9 1.3 slice_bitcast_fusion.12
  736.1 0.8 fusion.33
  736.9 8.3 %all-to-all-done.1 = bf16[512,4,128]{2,0,1:T(8,128)(2,1)S(1)} async-done(((bf16[512,4,128]{2,0,1:T(8,128)(2,1)}), bf16[512,4,128]{2,0,1:T(8,128)(2,1)S(1)}, u32[]{:S(2)}, u32[]{:S(2)}) %all-to-all-start.1) | async-done | bytes 524320 | tf_op jit(solution)/shard_map/all_to_all | solution.py:1048
  745.2 1.0 convert_element_type.145
  746.2 1.9 copy.57
  (100 shorter events, 5.3 us)
Async XLA Ops:
  0.7 44.7 %copy-start.25 = (bf16[256,160]{0,1:T(8,128)(2,1)S(1)}, bf16[256,160]{0,1:T(8,128)(2,1)}, u32[]{:S(2)}) copy-start(bf16[256,160]{0,1:T(8,128)(2,1)} %param.20) | copy-start | bytes 245764
  0.7 44.7 %copy-start.24 = (bf16[256,160]{0,1:T(8,128)(2,1)S(1)}, bf16[256,160]{0,1:T(8,128)(2,1)}, u32[]{:S(2)}) copy-start(bf16[256,160]{0,1:T(8,128)(2,1)} %param.21) | copy-start | bytes 245764
  0.7 44.7 %copy-start.23 = (bf16[160,256]{1,0:T(8,128)(2,1)S(1)}, bf16[160,256]{1,0:T(8,128)(2,1)}, u32[]{:S(2)}) copy-start(bf16[160,256]{1,0:T(8,128)(2,1)} %param.29) | copy-start | bytes 245764
  85.2 5.0 copy-start
  90.2 2.9 copy-start.7
  90.2 2.9 copy-start.9
  93.1 2.7 copy-start.26
  108.7 29.6 %copy-start.11 = (bf16[1,4,160,2048]{3,2,1,0:T(8,128)(2,1)S(1)}, bf16[1,4,160,2048]{3,2,1,0:T(8,128)(2,1)}, u32[]{:S(2)}) copy-start(bf16[1,4,160,2048]{3,2,1,0:T(8,128)(2,1)} %get-tuple-element.111) | copy-start | bytes 7864324
  308.8 3.4 copy-start.3
  308.8 6.9 slice-start.2
  311.6 7.6 %copy-start.16 = (bf16[512,2048]{1,0:T(8,128)(2,1)}, bf16[512,2048]{1,0:T(8,128)(2,1)S(1)}, u32[]{:S(2)}) copy-start(bf16[512,2048]{1,0:T(8,128)(2,1)S(1)} %multiply_convert_fusion) | copy-start | bytes 6291460
  312.2 3.5 slice-start.3
  312.2 3.5 copy-start.5
  312.2 7.0 slice-start
  315.7 3.5 slice-start.1
  336.7 1.2 copy-start.32
  369.2 362.2 %all-to-all-start = ((bf16[512,4,128]{2,0,1:T(8,128)(2,1)}), bf16[512,4,128]{2,0,1:T(8,128)(2,1)}, u32[]{:S(2)}, u32[]{:S(2)}) async-start(bf16[512,4,128]{2,0,1:T(8,128)(2,1)} %copy_bitcast_fusion.1), calls=%async_computation | async-start | bytes 1048576 | tf_op jit(solution)/shard_map/all_to_all | solution.py:1048
  373.4 6.2 copy-start.2
  373.4 6.2 copy-start.30
  379.6 52.3 %copy-start.6 = (bf16[512,2048]{1,0:T(8,128)(2,1)S(1)}, bf16[512,2048]{1,0:T(8,128)(2,1)}, u32[]{:S(2)}) copy-start(bf16[512,2048]{1,0:T(8,128)(2,1)} %gather_tokens.1) | copy-start | bytes 6291460
  431.9 5.1 copy-start.12
  431.9 5.1 copy-start.28
  437.0 2.9 copy-start.17
  437.0 2.9 copy-start.34
  439.9 5.4 copy-start.31
  485.8 4.4 copy-start.10
  485.8 4.4 copy-start.22
  490.2 1.8 copy-start.33
  492.1 5.4 copy-start.21
  497.5 3.2 copy-start.1
  497.5 5.8 copy-start.29
  500.6 2.5 copy-start.27
  500.6 2.6 copy-start.8
  508.4 43.6 %copy-start.15 = (bf16[640,2048]{1,0:T(8,128)(2,1)S(1)}, bf16[640,2048]{1,0:T(8,128)(2,1)}, u32[]{:S(2)}) copy-start(bf16[640,2048]{1,0:T(8,128)(2,1)} %convolution_convert_fusion.4) | copy-start | bytes 7864324
  508.6 43.5 %copy-start.13 = (bf16[640,2048]{1,0:T(8,128)(2,1)S(1)}, bf16[640,2048]{1,0:T(8,128)(2,1)}, u32[]{:S(2)}) copy-start(bf16[640,2048]{1,0:T(8,128)(2,1)} %convolution_convert_fusion.3) | copy-start | bytes 7864324
  508.6 43.5 %copy-start.14 = (bf16[640,2048]{1,0:T(8,128)(2,1)S(1)}, bf16[640,2048]{1,0:T(8,128)(2,1)}, u32[]{:S(2)}) copy-start(bf16[640,2048]{1,0:T(8,128)(2,1)} %convolution_convert_fusion.5) | copy-start | bytes 7864324
  694.3 35.0 %copy-start.4 = (f32[512,512]{1,0:T(8,128)S(1)}, f32[512,512]{1,0:T(8,128)}, u32[]{:S(2)}) copy-start(f32[512,512]{1,0:T(8,128)} %ownsum.3) | copy-start | bytes 3145732
  694.3 35.0 %copy-start.20 = (f32[512,512]{1,0:T(8,128)S(1)}, f32[512,512]{1,0:T(8,128)}, u32[]{:S(2)}) copy-start(f32[512,512]{1,0:T(8,128)} %get-tuple-element.50) | copy-start | bytes 3145732
  729.3 6.8 copy-start.18
  729.3 18.8 %copy-start.19 = (f32[384,256]{1,0:T(8,128)S(1)}, f32[384,256]{1,0:T(8,128)}, u32[]{:S(2)}) copy-start(f32[384,256]{1,0:T(8,128)} %sum_grads.7) | copy-start | bytes 1179652
  731.4 13.8 %all-to-all-start.1 = ((bf16[512,4,128]{2,0,1:T(8,128)(2,1)}), bf16[512,4,128]{2,0,1:T(8,128)(2,1)S(1)}, u32[]{:S(2)}, u32[]{:S(2)}) async-start(bf16[512,4,128]{2,0,1:T(8,128)(2,1)} %copy_bitcast_fusion), calls=%async_computation.1 | async-start | bytes 1048576 | tf_op jit(solution)/shard_map/all_to_all | solution.py:1048

commit v2 on v0

v2 whole, which is shorter than its diff:
```python
import jax
import jax.numpy as jnp
from jax import lax
from jax.experimental import pallas as pl
from jax.experimental.pallas import tpu as pltpu
from jax.sharding import Mesh, PartitionSpec as P

D = 2048
CONV = 4
EPS = 1e-06
TOK = 512
CH = 640
HW = 160
MESH = pl.DeviceIdType.MESH
SEQ = ("ylo", "x")
HEAD = ("z", "yhi", "core")
QUAD = ("yhi", "core")
PLANE = ("ylo", "x", "yhi", "core")
bf = jnp.bfloat16
f32 = jnp.float32
VMEM = pl.BlockSpec(memory_space=pltpu.VMEM)
ANY = pl.BlockSpec(memory_space=pl.ANY)


def shape(dims, dtype):
    return jax.ShapeDtypeStruct(dims, dtype)


def params(cid):
    return pltpu.CompilerParams(
        collective_id=cid, has_side_effects=True, vmem_limit_bytes=56 * 2**20
    )


def quad_device(index):
    return {"yhi": index // 2, "core": lax.rem(index, 2)}


def plane_device(block):
    return {
        "ylo": block // 16,
        "x": lax.rem(block // 4, 4),
        "yhi": lax.rem(block // 2, 2),
        "core": lax.rem(block, 2),
    }


def meet(devices):
    barrier = pltpu.get_barrier_semaphore()
    for device in devices:
        pl.semaphore_signal(barrier, inc=1, device_id=device, device_id_type=MESH)
    pl.semaphore_wait(barrier, len(devices))


def place():
    ylo, x, yhi, core = (lax.axis_index(n) for n in ("ylo", "x", "yhi", "core"))
    return ylo, x, yhi, core

def x_device(i):
    return {"x": i}

def y_device(i):
    return {"yhi": i // 2, "ylo": lax.rem(i, 2)}

def around(i):
    return lax.rem(i + 1, 4), lax.rem(i + 3, 4), lax.rem(i + 2, 4)

def plane_neighbours():
    ylo, x, yhi, core = place()
    y = yhi * 2 + ylo
    xr, xl, _ = around(x)
    yr, yl, _ = around(y)
    return [x_device(xr), x_device(xl), y_device(yr), y_device(yl), {"core": 1 - core}]

class Sender:
    def __init__(self, send, recv):
        self.send, self.recv, self.all = send, recv, []

    def __call__(self, source, target, device):
        i = len(self.all)
        copy = pltpu.make_async_remote_copy(
            src_ref=source,
            dst_ref=target,
            send_sem=self.send.at[i],
            recv_sem=self.recv.at[i],
            device_id=device,
            device_id_type=MESH,
        )
        copy.start()
        self.all.append(copy)
        return copy

    def drain(self, skip=None):
        for copy in self.all:
            if copy is not skip:
                copy.wait_send()


class Keeper:
    def __init__(self, done):
        self.done, self.count, self.open = done, 0, []

    def __call__(self, source, target):
        copy = pltpu.make_async_copy(source, target, self.done.at[self.count])
        copy.start()
        self.count += 1
        self.open.append(copy)
        return copy

    def wait(self, copy):
        self.open = [c for c in self.open if c is not copy]
        copy.wait()

    def drain(self):
        for copy in self.open:
            copy.wait()


def semaphores(count):
    return [pltpu.SemaphoreType.DMA((count,)), pltpu.SemaphoreType.DMA((count,))]


def got(copies):
    for copy in copies:
        copy.wait_recv()


def step(*plans):
    for plan in plans:
        next(plan, None)


def finish(*plans):
    for plan in plans:
        for _ in plan:
            pass


def z_columns(block):
    return pl.ds(pl.multiple_of(block * 512, 512), 512)


def ring_gather(full, put):
    z = lax.axis_index("z")
    right, left, _ = around(z)
    half = full.shape[0] // 2

    def start(row, block, to):
        part = full.at[pl.ds(row, half), z_columns(block)]
        return put(part, part, {"z": to})

    c0 = start(0, z, right)
    c1 = start(half, z, left)
    c2 = start(half, z, right)
    c3 = start(0, z, left)
    yield
    c0.wait_recv()
    c4 = start(0, left, right)
    c1.wait_recv()
    c5 = start(half, right, left)
    yield
    got([c2, c3, c4, c5])


def ring_sum(part, out, came, sent, put, produce=lambda block: None):
    z = lax.axis_index("z")
    right, left, far = around(z)
    half = part.shape[0] // 2
    lo, hi = pl.ds(0, half), pl.ds(half, half)
    cols = z_columns

    def start(i, source, to):
        return put(source, came.at[i], {"z": to})

    produce(far)
    c0 = start(0, part.at[lo, cols(far)], right)
    c1 = start(1, part.at[hi, cols(far)], left)
    produce(right)
    c2 = start(2, part.at[hi, cols(right)], right)
    produce(left)
    c3 = start(3, part.at[lo, cols(left)], left)
    produce(z)
    yield
    c0.wait_recv()
    sent[0] = (came[0].astype(f32) + part[lo, cols(right)].astype(f32)).astype(bf)
    c4 = start(4, sent.at[0], right)
    c1.wait_recv()
    sent[1] = (came[1].astype(f32) + part[hi, cols(left)].astype(f32)).astype(bf)
    c5 = start(5, sent.at[1], left)
    yield
    got([c3, c4])
    out[lo, :] = part[lo, cols(z)].astype(f32) + came[3].astype(f32) + came[4].astype(f32)
    got([c2, c5])
    out[hi, :] = part[hi, cols(z)].astype(f32) + came[2].astype(f32) + came[5].astype(f32)


def ring_scratch():
    return [pltpu.VMEM((6, TOK // 2, 512), bf), pltpu.VMEM((2, TOK // 2, 512), bf)]


def z_others():
    z = lax.axis_index("z")
    return [{"z": lax.rem(z + j, 4)} for j in (1, 2, 3)]


def quad_others():
    me = lax.axis_index("yhi") * 2 + lax.axis_index("core")
    return [quad_device(lax.rem(me + j, 4)) for j in (1, 2, 3)]


def quad_gather(tokens, full, put, keep):
    z = lax.axis_index("z")
    me = lax.axis_index("yhi") * 2 + lax.axis_index("core")
    mine = pl.ds(pl.multiple_of(z * 512 + me * 128, 128), 128)
    copies = []
    for j in (1, 2, 3):
        peer = lax.rem(me + j, 4)
        source = tokens.at[pl.ds(pl.multiple_of(peer * TOK, TOK), TOK), :]
        copies.append(put(source, full.at[:, mine], quad_device(peer)))
    own = keep(tokens.at[pl.ds(pl.multiple_of(me * TOK, TOK), TOK), :], full.at[:, mine])
    return copies, own


def token_gather(tokens, full, put, keep):
    copies, own = quad_gather(tokens, full, put, keep)
    yield
    got(copies)
    keep.wait(own)
    yield from ring_gather(full, put)


def quad_scatter(own, tokens, put):
    me = lax.axis_index("yhi") * 2 + lax.axis_index("core")
    rows = pl.ds(pl.multiple_of(me * TOK, TOK), TOK)
    copies = []
    for j in (1, 2, 3):
        peer = lax.rem(me + j, 4)
        source = own.at[:, pl.ds(pl.multiple_of(peer * 128, 128), 128)]
        copies.append(put(source, tokens.at[rows, :], quad_device(peer)))
    tokens[rows, :] = own[:, pl.ds(pl.multiple_of(me * 128, 128), 128)]
    return copies


GATHER_COPIES = 48
SUM_COPIES = 30


def resid_kernel(part, down, gate, full, own, down_sum, gate_sum, *rest):
    z = lax.axis_index("z")
    meet(z_others() + plane_neighbours())
    (came, sent), rest = rest[:2], rest[2:]
    a, b = rest[:SUM_SCRATCH], rest[SUM_SCRATCH : 2 * SUM_SCRATCH]
    put = Sender(*rest[2 * SUM_SCRATCH :])
    total = ring_sum(part, own, came, sent, put)
    plane_a = plane_sum(down, down_sum, a, put)
    plane_b = plane_sum(gate, gate_sum, b, put)
    step(total, plane_a, plane_b)
    step(total, plane_a)
    finish(total)
    full[:, z_columns(z)] = own[...].astype(bf)
    spread = ring_gather(full, put)
    step(spread, plane_b, plane_a, spread, plane_b, plane_a, plane_b, plane_a, plane_b)
    finish(spread, plane_a, plane_b)
    put.drain()


def resid_sum(part, down, gate):
    r = down.shape[1]
    return pl.pallas_call(
        resid_kernel,
        out_shape=(
            shape((TOK, D), bf),
            shape((TOK, 512), f32),
            shape((r, 256), f32),
            shape((r, 256), f32),
        ),
        in_specs=[VMEM] * 3,
        out_specs=[VMEM] * 4,
        scratch_shapes=ring_scratch()
        + sum_scratch(r)
        + sum_scratch(r)
        + semaphores(12 + 2 * SUM_COPIES),
        compiler_params=params(3),
        name="resid_sum",
    )(part, down, gate)


def cut(r):
    a = (r // 32) * 16
    a1 = ((a // 16 + 1) // 2) * 16
    b1 = (((r - a) // 16 + 1) // 2) * 16
    return a, a1, b1

def plane_gather(own, full, put, keep):
    k, r, _ = own.shape
    ylo, x, yhi, core = place()
    y = yhi * 2 + ylo
    xr, xl, xf = around(x)
    yr, yl, yf = around(y)
    a, a1, b1 = cut(r)
    top, bottom = (0, a), (a, r - a)
    top1, top2 = (0, a1), (a1, a - a1)
    bot1, bot2 = (a, b1), (a + b1, r - a - b1)

    def span(quarter, rows):
        return pl.ds(pl.multiple_of(quarter * r + rows[0], 16), rows[1])

    sib = {"core": 1 - core}
    def cols(lo, xx):
        return pl.ds(pl.multiple_of(lo * 1024 + xx * 256, 256), 256)
    def one(rows, yy, xx):
        return full.at[:, span((yy // 2) * 2 + core, rows), cols(lax.rem(yy, 2), xx)]
    def row(rows, yy):
        return full.at[:, span((yy // 2) * 2 + core, rows), pl.ds(pl.multiple_of(lax.rem(yy, 2) * 1024, 1024), 1024)]
    kept = keep(own, one((0, r), y, x))
    ha, hb = own.at[:, pl.ds(*top), :], own.at[:, pl.ds(*bottom), :]
    p = [put(ha, one(top, y, x), x_device(xr)), put(ha, one(top, y, x), x_device(xl)),
         put(hb, one(bottom, y, x), y_device(yr)), put(hb, one(bottom, y, x), y_device(yl))]
    yield
    got(p)
    keep.wait(kept)
    p = [put(one(top1, y, xl), one(top1, y, xl), x_device(xr)), put(one(top2, y, xr), one(top2, y, xr), x_device(xl)),
         put(one(bot1, yl, x), one(bot1, yl, x), y_device(yr)), put(one(bot2, yr, x), one(bot2, yr, x), y_device(yl))]
    yield
    got(p)
    def pieces(rows, xx):
        out = []
        for lo in (0, 1):
            for hi in (0, 1):
                out.append(full.at[:, span(2 * hi + core, rows), cols(lo, xx)])
        return out
    def send_row(rows, yy, device):
        return [put(row(rows, yy), row(rows, yy), device)]
    def send_col(rows, xx, device):
        return [put(s, s, device) for s in pieces(rows, xx)]
    p = send_row(top, y, y_device(yr)) + send_row(top, y, y_device(yl))
    p += send_col(bottom, x, x_device(xr)) + send_col(bottom, x, x_device(xl))
    s = send_row(top, y, sib) + send_col(bottom, x, sib)
    yield
    got(p)
    p = send_row(top1, yl, y_device(yr)) + send_row(top2, yr, y_device(yl))
    p += send_col(bot1, xl, x_device(xr)) + send_col(bot2, xr, x_device(xl))
    s += send_row(top, yl, sib) + send_row(top, yr, sib) + send_col(bottom, xl, sib) + send_col(bottom, xr, sib)
    yield
    got(p)
    s += send_row(top, yf, sib) + send_col(bottom, xf, sib)
    yield
    got(s)


def plane_sum(part, out, scratch, put):
    fold, ga, gb, ha, hb, sa, sb, ra2, rb2 = scratch
    _, r, _ = part.shape
    ylo, x, yhi, core = place()
    y = yhi * 2 + ylo
    xr, xl, xf = around(x)
    yr, yl, yf = around(y)
    a = -(-r // 64) * 32
    h, g = a // 2, (r - a) // 2
    sib = {"core": 1 - core}
    p = []
    for hi in (0, 1):
        p.append(put(part.at[2 * hi + 1 - core], fold.at[hi], sib))
    yield
    for hi in (0, 1):
        p[hi].wait_recv()
        def body(i, carry, hi=hi):
            rr = pl.ds(pl.multiple_of(i * 16, 16), 16)
            fold[hi, rr, :] = (fold[hi, rr, :].astype(f32) + part[2 * hi + core, rr, :].astype(f32)).astype(bf)
            return carry
        lax.fori_loop(0, r // 16, body, 0)
    def ycols(yy):
        return pl.ds(pl.multiple_of(lax.rem(yy, 2) * 1024, 1024), 1024)
    def a_block(yy, first):
        return fold.at[yy // 2, pl.ds(0 if first else h, h), ycols(yy)]
    def b_block(xx, first, l):
        return fold.at[:, pl.ds(a + (0 if first else g), g), pl.ds(pl.multiple_of(l * 1024 + xx * 256, 256), 256)]
    yR, yL, xR, xL = y_device(yr), y_device(yl), x_device(xr), x_device(xl)
    def sendb(i, xx, first, dev):
        return [put(b_block(xx, first, l), gb.at[i, l], dev) for l in (0, 1)]
    pa = [put(a_block(yf, True), ga.at[0], yR), put(a_block(yf, False), ga.at[1], yL)]
    pb = [sendb(0, xf, True, xR), sendb(1, xf, False, xL)]
    pa += [put(a_block(yr, False), ga.at[2], yR), put(a_block(yl, True), ga.at[3], yL)]
    pb += [sendb(2, xr, False, xR), sendb(3, xl, True, xL)]
    yield
    def add_a(dst, i, block, n):
        def body(j, carry):
            rr = pl.ds(pl.multiple_of(j * 16, 16), 16)
            dst[rr, :] = (ga[i, rr, :].astype(f32) + block[rr, :].astype(f32)).astype(bf)
            return carry
        lax.fori_loop(0, n // 16, body, 0)
    def add_b(dst, i, xx, first):
        for l in (0, 1):
            for hi in (0, 1):
                block = fold.at[hi, pl.ds(a + (0 if first else g), g), pl.ds(pl.multiple_of(l * 1024 + xx * 256, 256), 256)]
                def body(j, carry):
                    rr = pl.ds(pl.multiple_of(j * 16, 16), 16)
                    dst[l, hi, rr, :] = (gb[i, l, hi, rr, :].astype(f32) + block[rr, :].astype(f32)).astype(bf)
                    return carry
                lax.fori_loop(0, g // 16, body, 0)
    pa[0].wait_recv()
    add_a(sa.at[0], 0, a_block(yr, True), h)
    pa.append(put(sa.at[0], ga.at[4], yR))
    got(pb[0])
    add_b(sb.at[0], 0, xr, True)
    pb.append([put(sb.at[0], gb.at[4], xR)])
    pa[1].wait_recv()
    add_a(sa.at[1], 1, a_block(yl, False), h)
    pa.append(put(sa.at[1], ga.at[5], yL))
    got(pb[1])
    add_b(sb.at[1], 1, xl, False)
    pb.append([put(sb.at[1], gb.at[5], xL)])
    yield
    def fin_a(first, i, j):
        def body(n, carry):
            rr = pl.ds(pl.multiple_of(n * 16, 16), 16)
            block = a_block(y, first)
            ra2[pl.ds(pl.multiple_of((0 if first else h) + n * 16, 16), 16), :] = (
                block[rr, :].astype(f32) + ga[i, rr, :].astype(f32) + ga[j, rr, :].astype(f32)).astype(bf)
            return carry
        lax.fori_loop(0, h // 16, body, 0)
    def fin_b(first, i, j):
        for l in (0, 1):
            for hi in (0, 1):
                block = fold.at[hi, pl.ds(a + (0 if first else g), g), pl.ds(pl.multiple_of(l * 1024 + x * 256, 256), 256)]
                def body(n, carry):
                    rr = pl.ds(pl.multiple_of(n * 16, 16), 16)
                    rb2[l, hi, pl.ds(pl.multiple_of((0 if first else g) + n * 16, 16), 16), :] = (
                        block[rr, :].astype(f32) + gb[i, l, hi, rr, :].astype(f32) + gb[j, l, hi, rr, :].astype(f32)).astype(bf)
                    return carry
                lax.fori_loop(0, g // 16, body, 0)
    got([pa[3], pa[4]])
    fin_a(True, 3, 4)
    got([pa[2], pa[5]])
    fin_a(False, 2, 5)
    got(pb[3] + pb[4])
    fin_b(True, 3, 4)
    got(pb[2] + pb[5])
    fin_b(False, 2, 5)
    def a2(xx, first):
        return ra2.at[pl.ds(0 if first else h, h), pl.ds(pl.multiple_of(xx * 256, 256), 256)]
    def b2(yy, first):
        return rb2.at[lax.rem(yy, 2), yy // 2, pl.ds(0 if first else g, g), :]
    qa = [put(a2(xf, True), ha.at[0], xR), put(a2(xf, False), ha.at[1], xL), put(a2(xr, False), ha.at[2], xR), put(a2(xl, True), ha.at[3], xL)]
    qb = [put(b2(yf, True), hb.at[0], yR), put(b2(yf, False), hb.at[1], yL), put(b2(yr, False), hb.at[2], yR), put(b2(yl, True), hb.at[3], yL)]
    yield
    sa2, sb2 = ha.at[pl.ds(6, 2)], hb.at[pl.ds(6, 2)]
    qa[0].wait_recv()
    sa2[0] = (ha[0].astype(f32) + a2(xr, True)[...].astype(f32)).astype(bf)
    qa.append(put(sa2.at[0], ha.at[4], xR))
    qb[0].wait_recv()
    sb2[0] = (hb[0].astype(f32) + b2(yr, True)[...].astype(f32)).astype(bf)
    qb.append(put(sb2.at[0], hb.at[4], yR))
    qa[1].wait_recv()
    sa2[1] = (ha[1].astype(f32) + a2(xl, False)[...].astype(f32)).astype(bf)
    qa.append(put(sa2.at[1], ha.at[5], xL))
    qb[1].wait_recv()
    sb2[1] = (hb[1].astype(f32) + b2(yl, False)[...].astype(f32)).astype(bf)
    qb.append(put(sb2.at[1], hb.at[5], yL))
    yield
    got(qa[2:] + qb[2:])
    def w(v): return v.astype(f32)
    out[0:h, :] = w(a2(x, True)[...]) + w(ha[3]) + w(ha[4])
    out[h:a, :] = w(a2(x, False)[...]) + w(ha[2]) + w(ha[5])
    out[a:a + g, :] = w(b2(y, True)[...]) + w(hb[3]) + w(hb[4])
    out[a + g:, :] = w(b2(y, False)[...]) + w(hb[2]) + w(hb[5])


SUM_SCRATCH = 9


def sum_scratch(r):
    a = -(-r // 64) * 32
    h, g = a // 2, (r - a) // 2
    V = pltpu.VMEM
    return [V((2, r, 2048), bf), V((6, h, 1024), bf), V((6, 2, 2, g, 256), bf), V((8, h, 256), bf), V((8, g, 256), bf),
            V((2, h, 1024), bf), V((2, 2, 2, g, 256), bf), V((a, 1024), bf), V((2, 2, r - a, 256), bf)]


def small_sums(blocks, gains, small, gain, scratch, put):
    zgot, qgot, qgain, rgot, rgain, mine = scratch
    z = lax.axis_index("z")
    me = lax.axis_index("yhi") * 2 + lax.axis_index("core")
    row = lax.axis_index("ylo") * 4 + lax.axis_index("x")
    zs, qs = [], []
    for j in (1, 2, 3):
        to = lax.rem(z + j, 4)
        zs.append(put(gains.at[to], zgot.at[j - 1], {"z": to}))
    for j in (1, 2, 3):
        to = lax.rem(me + j, 4)
        qs.append(put(blocks.at[to], qgot.at[j - 1], quad_device(to)))
    yield
    got(zs)
    qgain[3] = gains[z] + zgot[0] + zgot[1] + zgot[2]
    for j in (1, 2, 3):
        to = lax.rem(me + j, 4)
        qs.append(put(qgain.at[3, to], qgain.at[j - 1, 0], quad_device(to)))
    got(qs)
    mine[...] = blocks[me] + qgot[0] + qgot[1] + qgot[2]
    rgain[7] = qgain[3, me] + qgain[0, 0] + qgain[1, 0] + qgain[2, 0]
    rs = []

    def seq(j):
        to = lax.rem(row + j, 8)
        return to, {"ylo": to // 4, "x": lax.rem(to, 4)}

    for j in range(1, 8):
        to, device = seq(j)
        rs.append(put(mine.at[pl.ds(pl.multiple_of(to * 48, 8), 48), :], rgot.at[j - 1], device))
        rs.append(put(rgain.at[7], rgain.at[j - 1], device))
    yield
    got(rs)
    own = pl.ds(pl.multiple_of(row * 48, 8), 48)
    total = mine[own, :]
    gain_total = rgain[7]
    for j in range(7):
        total = total + rgot[j]
        gain_total = gain_total + rgain[j]
    small[own, :] = total
    gain[...] = gain_total
    ag = []
    for j in range(1, 8):
        _, device = seq(j)
        ag.append(put(small.at[own, :], small.at[own, :], device))
    yield
    got(ag)


SMALL_SCRATCH = 6


def small_scratch():
    return [
        pltpu.VMEM((3, 4, 8, 128), f32),
        pltpu.VMEM((3, 384, HW), f32),
        pltpu.VMEM((4, 4, 8, 128), f32),
        pltpu.VMEM((7, 48, HW), f32),
        pltpu.VMEM((8, 8, 128), f32),
        pltpu.VMEM((384, HW), f32),
    ]


def last_kernel(part, dz, rec, blocks, gains, grad_in, rec_sum, small, gain, own, low, *rest):
    meet(z_others() + plane_neighbours() + line_devices())
    (came, sent), rest = rest[:2], rest[2:]
    plane_refs, rest = rest[:SUM_SCRATCH], rest[SUM_SCRATCH:]
    small_refs, rest = rest[:SMALL_SCRATCH], rest[SMALL_SCRATCH:]
    put = Sender(*rest)
    total = ring_sum(part, own, came, sent, put)
    little = small_sums(blocks, gains, small, gain, small_refs, put)
    plane = plane_sum(rec, rec_sum, plane_refs, put)
    step(total, little, plane)
    step(total, plane, little)
    finish(total)
    low[...] = (own[...] + dz[...]).astype(bf)
    back = quad_scatter(low, grad_in, put)
    step(plane, little)
    finish(plane, little)
    got(back)
    put.drain()


def last_sums(part, dz, rec, blocks, gains):
    r = rec.shape[1]
    return pl.pallas_call(
        last_kernel,
        out_shape=(
            shape((4 * TOK, 128), bf),
            shape((r, 256), f32),
            shape((384, HW), f32),
            shape((8, 128), f32),
        ),
        in_specs=[VMEM] * 5,
        out_specs=[VMEM] * 4,
        scratch_shapes=[pltpu.VMEM((TOK, 512), f32), pltpu.VMEM((TOK, 512), bf)]
        + ring_scratch()
        + sum_scratch(r)
        + small_scratch()
        + semaphores(6 + 3 + SUM_COPIES + 30),
        compiler_params=params(5),
        name="last_sums",
    )(part, dz, rec, blocks, gains)


def line_devices():
    ylo, x = lax.axis_index("ylo"), lax.axis_index("x")
    row = ylo * 4 + x
    rows = [
        {"ylo": lax.rem(row + j, 8) // 4, "x": lax.rem(row + j, 4)} for j in range(1, 8)
    ]
    return quad_others() + rows


def my_block():
    row = lax.axis_index("ylo") * 4 + lax.axis_index("x")
    return row * 4 + lax.axis_index("yhi") * 2 + lax.axis_index("core")


def line_prefix(mine, quad, rows, total, put, backward):
    me = lax.axis_index("yhi") * 2 + lax.axis_index("core")
    row = lax.axis_index("ylo") * 4 + lax.axis_index("x")
    copies = []
    for j in (1, 2, 3):
        copies.append(put(mine, quad.at[me], quad_device(lax.rem(me + j, 4))))
    quad[me] = mine[...]
    got(copies)
    ones = jnp.ones((1, CH), f32)
    zeros = jnp.zeros((1, CH), f32)
    prod, end, prod_all, end_all = ones, zeros, ones, zeros
    for turn in range(4):
        q = 3 - turn if backward else turn
        a, b = quad[q, 0:1, :], quad[q, 1:2, :]
        end_all = a * end_all + b
        prod_all = a * prod_all
        take = (q > me) if backward else (q < me)
        end = jnp.where(take, a * end + b, end)
        prod = jnp.where(take, a * prod, prod)
    total[0:1, :] = prod_all
    total[1:2, :] = end_all
    copies = []
    for j in range(1, 8):
        other = lax.rem(row + j, 8)
        copies.append(put(total, rows.at[row], {"ylo": other // 4, "x": lax.rem(other, 4)}))
    rows[row] = total[...]
    got(copies)
    came = zeros
    for turn in range(8):
        r = 7 - turn if backward else turn
        a, b = rows[r, 0:1, :], rows[r, 1:2, :]
        take = (r > row) if backward else (r < row)
        came = jnp.where(take, a * came + b, came)
    return prod * came + end


def pack_square(weight):
    tail = jnp.pad(weight[:, 128:], ((0, 32), (0, 0))).reshape(4, 48, 32)
    return jnp.concatenate([weight[:, :128], tail.transpose(1, 0, 2).reshape(48, 128)], axis=0)


def unpack_square(packed):
    tail = packed[160:208].reshape(48, 4, 32).transpose(1, 0, 2).reshape(192, 32)[:HW]
    return jnp.concatenate([packed[:HW], tail], axis=1)


TAILS = ((0, 48), (48, 48), (96, 48), (144, 16))
SQUARE = 208
PACKED = 2 * SQUARE + 32


def split(values):
    high = values.astype(bf)
    return high, (values - high.astype(f32)).astype(bf)


def dot3(a, b, dims):
    (ah, al), (bh, bl) = a, b

    def one(p, q):
        return lax.dot_general(p, q, (dims, ((), ())), preferred_element_type=f32)

    return one(ah, bh) + (one(al, bh) + one(ah, bl))


def minus_expm1(v):
    near = -v * (
        1.0
        + v * (1 / 2) * (1.0 + v * (1 / 3) * (1.0 + v * (1 / 4) * (1.0 + v * (1 / 5) * (1.0 + v * (1 / 6)))))
    )
    return jnp.where(v > -0.3, near, 1.0 - jnp.exp(v))


def gelu_parts(v):
    cdf = 0.5 * (1.0 + lax.erf(v * 0.7071067811865476))
    pdf = 0.3989422804014327 * jnp.exp(-0.5 * v * v)
    return v * cdf, cdf + v * pdf


def shifted(values, by, fill, reverse):
    rows = lax.broadcasted_iota(jnp.int32, values.shape, 0)
    size = values.shape[0]
    if reverse:
        return jnp.where(rows < size - by, pltpu.roll(values, size - by, 0), fill)
    return jnp.where(rows >= by, pltpu.roll(values, by, 0), fill)


def behind(near, by):
    return near[8:24, :] if by == 0 else pltpu.roll(near, by, 0)[8:24, :]


def ahead(near, by):
    size = near.shape[0]
    return pltpu.roll(near, size - by, 0)[0 : size - 8, :]


def scan8(a, b, reverse):
    for by in (1, 2, 4):
        b = b + a * shifted(b, by, 0.0, reverse)
        a = a * shifted(a, by, 1.0, reverse)
    return a, b


def loop(count, body):
    def one(i, carry):
        body(i)
        return carry

    lax.fori_loop(0, count, one, 0)


def front_kernel(
    tokens, cotangent, packed, norms, own_rec, own_gate, own_up, own_down,
    x_out, n_out, xb_out, yb_out, c_out, rate_out, gin_out, a_out, m_out, h_out, hy_out, ext_out, hi_out, lo_out,
    mix_out, own_out, cot, rec_out, w_gate, w_up, w_down,
    inv, gains, vec, state_in, total_a,
    full, normed, weights, params_all, norms_all,
    xb, yb, c, rate, gin, a, m, h, hy, ext, gate_hi, gate_lo, pre, prod, part, mixed, mix_own,
    halo, mine, quad, rows, total, came_z, sent_z, send, recv, done,
):
    z = lax.axis_index("z")
    me = lax.axis_index("yhi") * 2 + lax.axis_index("core")
    block = my_block()
    after, before = lax.rem(block + 1, 32), lax.rem(block + 31, 32)
    meet(
        line_devices()
        + [plane_device(after), plane_device(before)]
        + plane_neighbours()
        + z_others()
    )
    put = Sender(send, recv)
    keep = Keeper(done)
    params_all[me] = packed[...]
    tokens_in = token_gather(tokens, full, put, keep)
    plane = plane_gather(own_rec, weights, put, keep)
    step(tokens_in, plane)
    small = []
    for j in (1, 2, 3):
        small.append(put(norms, norms_all.at[z, me], quad_device(lax.rem(me + j, 4))))
    norms_all[z, me] = norms[...]
    gate_hi[...] = jnp.zeros((CH, 2 * CH), bf)
    gate_lo[...] = jnp.zeros((CH, 2 * CH), bf)
    step(plane, tokens_in)
    got(small)
    small = []
    for j in (1, 2, 3):
        small.append(put(norms_all.at[z], norms_all.at[z], {"z": lax.rem(z + j, 4)}))
    step(plane, tokens_in)
    got(small)
    for i in range(4):
        for j in range(4):
            gains[:, 128 * (4 * i + j) : 128 * (4 * i + j + 1)] = norms_all[i, j]
    step(plane)
    finish(tokens_in)
    keep(full, x_out)
    other = token_gather(cotangent, cot, put, keep)
    plane_a = plane_gather(own_gate, w_gate, put, keep)
    plane_b = plane_gather(own_up, w_up, put, keep)
    plane_c = plane_gather(own_down, w_down, put, keep)
    core, yhi = lax.axis_index("core"), lax.axis_index("yhi")
    own_params = params_all.at[me]
    near = put(own_params, own_params, {"core": 1 - core})
    across = put(own_params, own_params, {"yhi": 1 - yhi})
    step(plane, other, plane_a)

    def norm(i):
        r = pl.ds(pl.multiple_of(i * 16, 16), 16)
        values = full[r, :].astype(f32)
        mean = jnp.sum(values * values, axis=1, keepdims=True) * (1.0 / D)
        scale = lax.rsqrt(mean + EPS)
        inv[r, :] = jnp.broadcast_to(scale, (16, 128))
        normed[r, :] = (values * scale * gains[0:1, :]).astype(bf)

    loop(TOK // 16, norm)
    keep(normed, n_out)
    finish(plane)
    keep(weights, rec_out)
    across.wait_recv()
    peer_params = params_all.at[lax.rem(me + 2, 4)]
    passed = put(peer_params, peer_params, {"core": 1 - core})
    step(plane_a, other)
    for i, into in ((0, xb), (1, yb)):
        for at, width in ((0, 256), (256, 256), (512, 128)):
            into[:, at : at + width] = lax.dot_general(
                normed[...],
                weights[i, at : at + width, :],
                (((1,), (1,)), ((), ())),
                preferred_element_type=f32,
            )
        if i == 0:
            halo_out = pl.ds(TOK - 16, 16)
            hy[halo_out, :] = xb[halo_out, :].astype(bf)
            edge = put(hy.at[halo_out, :], halo, plane_device(after))
            step(plane_a, plane_b)
    keep(xb, xb_out)
    keep(yb, yb_out)
    step(other)

    def widen(i):
        r = pl.multiple_of(i * 16, 16)
        ext[pl.ds(pl.multiple_of(8 + r, 8), 16), :] = xb[pl.ds(r, 16), :].astype(bf).astype(f32)

    loop(TOK // 16, widen)
    got([near, passed])
    for i in range(4):
        there = HW * i
        vec[:, there : there + 128] = params_all[i, 2 * SQUARE : 2 * SQUARE + 16, :]
        vec[:, there + 128 : there + HW] = params_all[i, 2 * SQUARE + 16 : PACKED, 0:32]
        for k in (0, 1):
            top = SQUARE * k
            high, low = split(params_all[i, top : top + HW, :])
            over = CH * k + HW * i
            gate_hi[there : there + HW, over : over + 128] = high
            gate_lo[there : there + HW, over : over + 128] = low
            for j, (at, size) in enumerate(TAILS):
                high, low = split(params_all[i, top + HW : top + HW + size, 32 * j : 32 * j + 32])
                rows_here = slice(there + at, there + at + size)
                gate_hi[rows_here, over + 128 : over + HW] = high
                gate_lo[rows_here, over + 128 : over + HW] = low
    keep(gate_hi, hi_out)
    keep(gate_lo, lo_out)
    edge.wait_recv()
    ext[0:8, :] = jnp.where(block > 0, halo[8:16, :].astype(f32), 0.0)

    def conv(i):
        r = i * 16
        near = ext[pl.ds(pl.multiple_of(r, 16), 24), :]
        acc = vec[4:5, :] + vec[0:1, :] * near[8:24, :]
        for k in (1, 2, 3):
            acc = acc + vec[k : k + 1, :] * behind(near, k)
        c[pl.ds(pl.multiple_of(r, 16), 16), :] = acc

    loop(TOK // 16, conv)
    keep(ext, ext_out)
    keep(c, c_out)
    step(plane_b)

    def gates(i):
        r = pl.ds(pl.multiple_of(i * 128, 128), 128)
        pre[r, :] = dot3(split(c[r, :]), (gate_hi[...], gate_lo[...]), ((1,), (0,)))

    loop(TOK // 128, gates)
    step(plane_a, other, plane_b, plane_c)

    def point(i, carry):
        prod_in, state = carry
        r = pl.ds(pl.multiple_of(i * 8, 8), 8)
        rr = jax.nn.sigmoid(pre[r, 0:CH] + vec[5:6, :])
        gg = jax.nn.sigmoid(pre[r, CH:] + vec[6:7, :])
        log_a = -8.0 * rr * vec[7:8, :]
        aa = jnp.exp(log_a)
        mm = jnp.sqrt(minus_expm1(2.0 * log_a))
        rate[r, :] = rr
        gin[r, :] = gg
        a[r, :] = aa
        m[r, :] = mm
        pa, hb = scan8(aa, mm * gg * c[r, :], False)
        hb = hb + pa * state
        pa = pa * prod_in
        h[r, :] = hb
        prod[r, :] = pa
        return pa[7:8, :], hb[7:8, :]

    last = (jnp.ones((1, CH), f32), jnp.zeros((1, CH), f32))
    last = lax.fori_loop(0, TOK // 16, point, last)
    step(plane_a, plane_c)
    last = lax.fori_loop(TOK // 16, TOK // 8, point, last)
    for source, target in ((rate, rate_out), (gin, gin_out), (a, a_out), (m, m_out)):
        keep(source, target)
    mine[...] = jnp.zeros((8, CH), f32)
    total[...] = jnp.zeros((8, CH), f32)
    mine[0:1, :] = last[0]
    mine[1:2, :] = last[1]
    came = line_prefix(mine, quad, rows, total, put, False)
    state_in[...] = jnp.broadcast_to(came, (8, CH))
    total_a[...] = jnp.broadcast_to(last[0], (8, CH))
    step(plane_b, plane_c)
    finish(plane_a, other)
    edge.wait_send()

    def complete(i):
        r = pl.ds(pl.multiple_of(i * 16, 16), 16)
        hh = h[r, :] + prod[r, :] * came
        h[r, :] = hh
        hy[r, :] = (hh * gelu_parts(yb[r, :])[0]).astype(bf)

    loop(TOK // 16, complete)
    keep(h, h_out)
    keep(hy, hy_out)

    def produce(at):
        part[:, z_columns(at)] = jnp.dot(
            hy[...], weights[2, :, z_columns(at)], preferred_element_type=f32
        ).astype(bf)

    whole = ring_sum(part, mix_own, came_z, sent_z, put, produce)
    step(whole, plane_b, whole, plane_c)
    finish(whole)
    mixed[:, z_columns(z)] = mix_own[...].astype(bf)
    keep(mix_own, own_out)
    spread = ring_gather(mixed, put)
    step(spread, plane_b, spread, plane_c)
    finish(spread)
    keep(mixed, mix_out)
    finish(plane_b, plane_c)
    put.drain(skip=edge)
    keep.drain()


def front(*operands):
    wide = shape((TOK, CH), f32)
    rows = shape((TOK, D), bf)
    mlp = shape((1, 1536, D), bf)
    gate = shape((CH, 2 * CH), bf)
    out = (
        rows, rows, wide, wide, wide, wide, wide, wide, wide, wide,
        shape((TOK, CH), bf), shape((TOK + 8, CH), f32), gate, gate,
        rows, shape((TOK, 512), f32), rows, shape((3, CH, D), bf), mlp, mlp, mlp,
    )
    little = (
        shape((TOK, 128), f32), shape((8, D), f32), shape((16, CH), f32),
        shape((8, CH), f32), shape((8, CH), f32),
    )
    tall = pltpu.VMEM((TOK, CH), f32)
    return pl.pallas_call(
        front_kernel,
        out_shape=out + little,
        in_specs=[VMEM] * 4 + [ANY] * 4,
        out_specs=[ANY] * len(out) + [VMEM] * len(little),
        scratch_shapes=[
            pltpu.VMEM((TOK, D), bf),
            pltpu.VMEM((TOK, D), bf),
            pltpu.VMEM((3, CH, D), bf),
            pltpu.VMEM((4, PACKED, 128), f32),
            pltpu.VMEM((4, 4, 8, 128), f32),
            tall, tall, tall, tall, tall, tall, tall, tall,
            pltpu.VMEM((TOK, CH), bf),
            pltpu.VMEM((TOK + 8, CH), f32),
            pltpu.VMEM((CH, 2 * CH), bf),
            pltpu.VMEM((CH, 2 * CH), bf),
            pltpu.VMEM((TOK, 2 * CH), f32),
            tall,
            pltpu.VMEM((TOK, D), bf),
            pltpu.VMEM((TOK, D), bf),
            pltpu.VMEM((TOK, 512), f32),
            pltpu.VMEM((16, CH), bf),
            pltpu.VMEM((8, CH), f32),
            pltpu.VMEM((4, 8, CH), f32),
            pltpu.VMEM((8, 8, CH), f32),
            pltpu.VMEM((8, CH), f32),
        ]
        + ring_scratch()
        + semaphores(18 + 9 + 11 + 12 + 4 * GATHER_COPIES)
        + [pltpu.SemaphoreType.DMA((26,))],
        compiler_params=params(0),
        name="front",
    )(*operands)


def backward_kernel(
    dhy, yb, gate_hi, gate_lo, vec, c, rate, gin, a, m, h, ext, state_in, total_a,
    mlp_part, z_own, up,
    dxb, dyb, dgate, sums, block_out, up_sum,
    e, apad, hpad, q, prod, pri, dc, halo, mine, quad, rows, total, own, low, came_z, sent_z, *rest,
):
    block = my_block()
    after, before = lax.rem(block + 1, 32), lax.rem(block + 31, 32)
    meet(
        line_devices()
        + [plane_device(after), plane_device(before)]
        + plane_neighbours()
        + z_others()
    )
    put = Sender(*rest[SUM_SCRATCH:])
    whole = ring_sum(mlp_part, own, came_z, sent_z, put)
    plane = plane_sum(up, up_sum, rest[:SUM_SCRATCH], put)
    step(whole, plane)

    def direct(i):
        r = pl.ds(pl.multiple_of(i * 16, 16), 16)
        value, slope = gelu_parts(yb[r, :])
        grad = dhy[r, :]
        hh = h[r, :]
        e[r, :] = grad * value
        dyb[r, :] = (grad * hh * slope).astype(bf)
        apad[r, :] = a[r, :]
        hpad[pl.ds(pl.multiple_of(i * 16 + 8, 8), 16), :] = hh

    loop(TOK // 16, direct)
    apad[TOK : TOK + 8, :] = jnp.ones((8, CH), f32)
    hpad[0:8, :] = state_in[...]
    step(whole)

    def adjoint(i, carry):
        prod_in, state = carry
        r0 = TOK - 8 - i * 8
        r = pl.ds(pl.multiple_of(r0, 8), 8)
        next_a = ahead(apad[pl.ds(pl.multiple_of(r0, 8), 16), :], 1)
        pa, qb = scan8(next_a, e[r, :], True)
        qb = qb + pa * state
        pa = pa * prod_in
        q[r, :] = qb
        prod[r, :] = pa
        return pa[0:1, :], qb[0:1, :]

    last = lax.fori_loop(
        0, TOK // 8, adjoint, (jnp.ones((1, CH), f32), jnp.zeros((1, CH), f32))
    )
    mine[...] = jnp.zeros((8, CH), f32)
    total[...] = jnp.zeros((8, CH), f32)
    mine[0:1, :] = total_a[0:1, :]
    mine[1:2, :] = a[0:1, :] * last[1]
    came = line_prefix(mine, quad, rows, total, put, True)
    step(plane)

    def point(i, carry):
        s_rate, s_input, s_decay = carry
        r = pl.ds(pl.multiple_of(i * 8, 8), 8)
        qq = q[r, :] + prod[r, :] * came
        aa, rr, gg, mm, cc = a[r, :], rate[r, :], gin[r, :], m[r, :], c[r, :]
        earlier = pltpu.roll(hpad[pl.ds(pl.multiple_of(i * 8, 8), 16), :], 1, 0)[8:16, :]
        grad_log = aa * (qq * earlier - qq * gg * cc * aa / mm)
        pr = -8.0 * vec[7:8, :] * grad_log * rr * (1.0 - rr)
        pi = qq * mm * cc * gg * (1.0 - gg)
        pri[r, 0:CH] = pr
        pri[r, CH:] = pi
        dc[r, :] = qq * mm * gg
        return s_rate + pr, s_input + pi, s_decay + 8.0 * rr * vec[8:9, :] * grad_log

    none = jnp.zeros((8, CH), f32)
    s_rate, s_input, s_decay = lax.fori_loop(0, TOK // 8, point, (none, none, none))
    step(plane)

    def spread(i):
        r = pl.ds(pl.multiple_of(i * 128, 128), 128)
        dc[r, :] = dc[r, :] + dot3(split(pri[r, :]), (gate_hi[...], gate_lo[...]), ((1,), (1,)))

    loop(TOK // 128, spread)
    edge = put(dc.at[pl.ds(0, 8), :], halo, plane_device(before))
    finish(whole)
    low[...] = (own[...] + z_own[...]).astype(bf)
    back = quad_scatter(low, block_out, put)
    step(plane)
    dgate[...] = dot3(split(c[...]), split(pri[...]), ((0,), (0,)))
    step(plane)
    edge.wait_recv()
    dc[TOK : TOK + 8, :] = jnp.where(block < 31, halo[...], 0.0)

    def taps(i, carry):
        r = i * 16
        here = pl.ds(pl.multiple_of(r, 16), 16)
        later = dc[pl.ds(pl.multiple_of(r, 16), 24), :]
        near = ext[pl.ds(pl.multiple_of(r, 16), 24), :]
        dd = later[0:16, :]
        out = vec[0:1, :] * dd
        for k in (1, 2, 3):
            out = out + vec[k : k + 1, :] * ahead(later, k)
        dxb[here, :] = out.astype(bf)

        def fold(v):
            return v[0:8, :] + v[8:16, :]

        new = [carry[0] + fold(dd)]
        for k in range(4):
            new.append(carry[1 + k] + fold(dd * behind(near, k)))
        return tuple(new)

    s_bias, *s_taps = lax.fori_loop(0, TOK // 16, taps, (none,) * 5)

    def place_sum(row, value):
        sums[row : row + 1, :] = jnp.sum(value, axis=0, keepdims=True)

    for k in range(4):
        place_sum(k, s_taps[k])
    place_sum(4, s_bias)
    place_sum(5, s_rate)
    place_sum(6, s_input)
    place_sum(7, s_decay)
    finish(plane)
    got(back)
    put.drain()


def backward_scan(*operands):
    r = operands[-1].shape[1]
    return pl.pallas_call(
        backward_kernel,
        out_shape=(
            shape((TOK, CH), bf),
            shape((TOK, CH), bf),
            shape((CH, 2 * CH), f32),
            shape((8, CH), f32),
            shape((4 * TOK, 128), bf),
            shape((r, 256), f32),
        ),
        in_specs=[VMEM] * 17,
        out_specs=[VMEM] * 6,
        scratch_shapes=[
            pltpu.VMEM((TOK, CH), f32),
            pltpu.VMEM((TOK + 8, CH), f32),
            pltpu.VMEM((TOK + 8, CH), f32),
            pltpu.VMEM((TOK, CH), f32),
            pltpu.VMEM((TOK, CH), f32),
            pltpu.VMEM((TOK, 2 * CH), f32),
            pltpu.VMEM((TOK + 8, CH), f32),
            pltpu.VMEM((8, CH), f32),
            pltpu.VMEM((8, CH), f32),
            pltpu.VMEM((4, 8, CH), f32),
            pltpu.VMEM((8, 8, CH), f32),
            pltpu.VMEM((8, CH), f32),
            pltpu.VMEM((TOK, 512), f32),
            pltpu.VMEM((TOK, 512), bf),
        ]
        + ring_scratch()
        + sum_scratch(r)
        + semaphores(11 + 6 + 3 + SUM_COPIES),
        compiler_params=params(4),
        name="backward_scan",
    )(*operands)


def dot(p, q):
    return jnp.dot(p, q, preferred_element_type=f32)


def dot_t0(p, q):
    return lax.dot_general(p, q, (((0,), (0,)), ((), ())), preferred_element_type=f32)


def dot_t1(p, q):
    return lax.dot_general(p, q, (((1,), (1,)), ((), ())), preferred_element_type=f32)


def per_device(
    block_in, cotangent, norm_one, rec_in, rec_gate, conv_weight, conv_bias,
    rate_weight, rate_bias, input_weight, input_bias, decay_code, rec_out,
    norm_two, mlp_gate, mlp_up, mlp_down,
):
    decay = decay_code.astype(f32) / 256.0
    vectors = jnp.concatenate(
        [
            conv_weight,
            conv_bias[None],
            rate_bias[None],
            input_bias[None],
            jax.nn.softplus(-decay)[None],
            jax.nn.sigmoid(-decay)[None],
            jnp.zeros((7, HW), f32),
        ],
        axis=0,
    )
    packed = jnp.concatenate(
        [
            pack_square(rate_weight[0]),
            pack_square(input_weight[0]),
            vectors[:, :128],
            jnp.pad(vectors[:, 128:], ((0, 0), (0, 96))),
        ],
        axis=0,
    )
    norms = jnp.concatenate([norm_one[None], norm_two[None], jnp.zeros((6, 128), f32)], axis=0)
    (
        x_full, n_one, xb, yb, c, rate, gin, a, m, h, hy, ext, gate_hi, gate_lo,
        mix_full, mix_own, cot_full, w_rec, w_gate, w_up, w_down,
        inv_one, gains, vec, state_in, total_a,
    ) = front(
        block_in, cotangent, packed, norms,
        jnp.stack([rec_in.T, rec_gate.T, rec_out]), mlp_gate.T[None], mlp_up.T[None], mlp_down[None],
    )
    w_in, w_gate_rec, w_out = w_rec[0], w_rec[1], w_rec[2]
    w_gate, w_up, w_down = w_gate[0], w_up[0], w_down[0]
    gain_one, gain_two = gains[0:1], gains[1:2]
    inv_one = inv_one[:, :1]
    x_rows = x_full.astype(f32)
    z = lax.axis_index("z")
    x_own = lax.dynamic_slice(x_full, (0, z * 512), (TOK, 512)).astype(f32)
    z_rows = x_rows + mix_full.astype(f32)
    z_own = x_own + mix_own
    inv_two = lax.rsqrt(jnp.mean(z_rows * z_rows, axis=1, keepdims=True) + EPS)
    n_two = (z_rows * inv_two * gain_two).astype(bf)

    g = dot_t1(n_two, w_gate)
    u = dot_t1(n_two, w_up)
    gelu_g, slope_g = gelu_parts(g)
    act = (gelu_g * u).astype(bf)
    dact = dot_t1(cot_full, w_down)
    dg = (dact * u * slope_g).astype(bf)
    du = (dact * gelu_g).astype(bf)
    inner_two = jnp.sum(dg.astype(f32) * g + du.astype(f32) * u, axis=1, keepdims=True)
    dn_two = dot(dg, w_gate) + dot(du, w_up)
    step_two = dn_two * inv_two * gain_two - z_rows * (inv_two * inv_two * inner_two / D)
    gain_two_sums = jnp.sum(dn_two * z_rows * inv_two, axis=0)
    part_down = dot_t0(act, cot_full).astype(bf).reshape(4, 384, D)
    part_gate = dot_t0(dg, n_two).astype(bf).reshape(4, 384, D)
    part_up = dot_t0(du, n_two).astype(bf).reshape(4, 384, D)
    back_full, back_own, grad_down, grad_gate = resid_sum(
        step_two.astype(bf), part_down, part_gate
    )
    dmix = (cot_full.astype(f32) + back_full.astype(f32)).astype(bf)
    cot_own = lax.dynamic_slice(cot_full, (0, z * 512), (TOK, 512)).astype(f32)
    dz_own = cot_own + back_own

    dhy = dot_t1(dmix, w_out)
    dxb, dyb, dgate, sums, block_out, grad_up = backward_scan(
        dhy, yb, gate_hi, gate_lo, vec, c, rate, gin, a, m, h, ext, state_in, total_a,
        dot(act, w_down).astype(bf), z_own, part_up,
    )
    inner_one = jnp.sum(dxb.astype(f32) * xb + dyb.astype(f32) * yb, axis=1, keepdims=True)
    dn_one = dot(dxb, w_in) + dot(dyb, w_gate_rec)
    step_one = dn_one * inv_one * gain_one - x_rows * (inv_one * inv_one * inner_one / D)
    gain_one_sums = jnp.sum(dn_one * x_rows * inv_one, axis=0)
    part_rec = jnp.concatenate(
        [dot_t0(p, q).astype(bf).reshape(4, HW, D) for p, q in ((dxb, n_one), (dyb, n_one), (hy, dmix))],
        axis=1,
    )
    blocks = [
        jnp.concatenate(
            [
                dgate[HW * i : HW * (i + 1), HW * i : HW * (i + 1)],
                dgate[HW * i : HW * (i + 1), CH + HW * i : CH + HW * (i + 1)],
                sums[:, HW * i : HW * (i + 1)],
                jnp.zeros((56, HW), f32),
            ],
            axis=0,
        )
        for i in range(4)
    ]
    gains = jnp.stack([gain_one_sums.reshape(4, 4, 128), gain_two_sums.reshape(4, 4, 128)], axis=2)
    gains = jnp.concatenate([gains, jnp.zeros((4, 4, 6, 128), f32)], axis=2)
    grad_in, grad_rec, small, gain_sums = last_sums(
        step_one.astype(bf), dz_own, part_rec, jnp.stack(blocks), gains
    )
    grad_rec_in, grad_rec_gate, grad_out = grad_rec[:HW].T, grad_rec[HW : 2 * HW].T, grad_rec[2 * HW :]
    vector_grads = small[2 * HW : 2 * HW + 8]
    return (
        block_out,
        grad_in.astype(f32),
        gain_sums[0],
        grad_rec_in,
        grad_rec_gate,
        vector_grads[0:4],
        vector_grads[4],
        small[:HW][None],
        vector_grads[5],
        small[HW : 2 * HW][None],
        vector_grads[6],
        vector_grads[7],
        grad_out,
        gain_sums[1],
        grad_gate.T,
        grad_up.T,
        grad_down,
    )


def solution(mesh):
    fine = Mesh(mesh.devices.reshape(2, 4, 4, 2, 2), ("ylo", "x", "z", "yhi", "core"))
    both = P(SEQ, HEAD)
    swap = P(HEAD, SEQ)
    vector = P(HEAD)
    stack = P(HEAD, None, None)
    taps = P(None, HEAD)
    return jax.shard_map(
        per_device,
        mesh=fine,
        in_specs=(
            both, both, vector, both, both, taps, vector, stack, vector, stack, vector, vector,
            swap, vector, both, both, swap,
        ),
        out_specs=(
            both, both, vector, both, both, taps, vector, stack, vector, stack, vector, vector,
            swap, vector, both, both, swap,
        ),
        check_vma=False,
    )
```

time: 2590 us -> 469 us (0.18)
  local copies, waits for them, and re-layouts: 1110 us -> 27.5 us
  waiting for transfers between devices: 853 us -> 0 us
  Pallas kernels: 0 us -> 340 us
  blocking collectives: 287 us -> 0 us
  matrix products: 177 us -> 72.7 us
  other arithmetic: 125 us -> 21.1 us
    slice x140 -> x9, local copies, waits for them, and re-layouts: 632 us -> 9.33 us  [the longest x1 1.86 us: per_device(): grad_rec[2 * HW:]]
    reduce_scatter x10 -> x0, waiting for transfers between devices: 569 us -> none  [the longest x2 294 us: feature_sum(): lax.psum_scatter(partial_rows, 'head', scatter_dimension=1, tiled=True)]
    pad x80 -> x2, local copies, waits for them, and re-layouts: 395 us -> 0.02 us  [pack_square(): tail = jnp.pad(weight[:, 128:], ((0, 32), (0, 0))).reshape(4, 48, 32)]
    pallas_call x0 -> x4, Pallas kernels: none -> 340 us  [the longest x1 151 us: front(): pl.pallas_call(front_kernel, out_shape=out + little, in_specs=[VMEM] * 4...]
    all_gather x7 -> x0, waiting for transfers between devices: 206 us -> none  [the longest x2 81 us: grads_gather(): lax.all_gather(grad_rows.astype(jnp.bfloat16), 'head', axis=1, tiled=True)]
    all_gather x6 -> x0, blocking collectives: 146 us -> none  [the longest x3 53.3 us: prefix(): gathered = jax.tree.map(lambda a: lax.all_gather(a, axis), part)]
    psum x4 -> x0, blocking collectives: 141 us -> none  [the longest x2 73.6 us: norm_forward(): summed = lax.psum(jnp.sum(values * values, axis=1), 'head')]
    dot_general x24 -> x15, matrix products: 177 us -> 72.7 us  [the longest x4 26 us: dot_t1(): lax.dot_general(p, q, (((1,), (1,)), ((), ())), preferred_element_type=f32)]
  transfers between devices with their start and end apart: 20 -> 0, of which waited for: 12 -> 0; matrix products, arithmetic and copies ran while one was open for 32% -> 0% of each run, Pallas kernels for 0% -> 0%
where the time goes in v2:
time: 469 us; the launch traced here: 463 us
  Pallas kernels  340 us (72%)
  matrix products  72.7 us (16%)
  local copies, waits for them, and re-layouts  27.5 us (6%)
  other arithmetic  21.1 us (4%)
    pallas_call x1, Pallas kernels, front(): pl.pallas_call(front_kernel, out_shape=out + little, in_specs=[VMEM] * 4...  151 us
    pallas_call x1, Pallas kernels, last_sums(): pl.pallas_call(last_kernel, out_shape=(shape((4 * TOK, 128), bf), shape((...  70.4 us
    pallas_call x1, Pallas kernels, resid_sum(): pl.pallas_call(resid_kernel, out_shape=(shape((TOK, D), bf), shape((TOK,...  59.8 us
    pallas_call x1, Pallas kernels, backward_scan(): pl.pallas_call(backward_kernel, out_shape=(shape((TOK, CH), bf), shape((T...  58.7 us
    dot_general x4, matrix products, dot_t1(): lax.dot_general(p, q, (((1,), (1,)), ((), ())), preferred_element_type=f32)  26 us
    dot_general x5, matrix products, dot(): return jnp.dot(p, q, preferred_element_type=f32)  23.9 us
    dot_general x6, matrix products, dot_t0(): lax.dot_general(p, q, (((0,), (0,)), ((), ())), preferred_element_type=f32)  22.7 us
    unnamed x69, local copies, waits for them, and re-layouts  13.8 us

profile of v2, /device:TPU:0, one launch (start us, length us, event | category | flops | bytes accessed | tf_op | source)
XLA Modules:
  0.0 462.7 jit_solution(297346298902441916)
XLA Ops:
  0.7 0.1 pad.45.clone
  0.7 0.1 pad.36.clone
  0.8 0.7 add_divide_fusion
  1.5 1.3 maximum_maximum_fusion.1.norms
  2.9 0.8 concatenate.27
  3.6 0.9 slice.151
  4.5 0.1 copy.49
  4.6 0.1 copy.51
  4.7 0.9 slice.153
  5.6 0.1 copy.50
  5.7 0.1 copy.52
  5.8 1.8 copy.53
  7.5 1.7 copy.54
  9.3 0.9 slice_dynamic-update-slice_fusion.1
  10.2 0.9 slice_dynamic-update-slice_fusion
  11.1 1.8 pad_maximum_fusion.2.own_rec
  12.9 151.0 %front.1 = (bf16[512,2048]{1,0:T(8,128)(2,1)}, bf16[512,2048]{1,0:T(8,128)(2,1)}, f32[512,640]{1,0:T(8,128)}, f32[512,640]{1,0:T(8,128)}, f32[512,640]{1,0:T(8,1...) custom-call(bf16[2048,128]{1,0:T(8,128)(2,1)} %tokens.1, ...), custom_call_target="tpu_custom_call" | custom-call | tf_op jit(solution)/shard_map/front/pallas_call | solution.py:923
  163.9 1.0 fusion.40
  165.0 3.2 multiply_reduce_fusion.1
  168.2 1.1 multiply_convert_fusion
  169.4 1.6 copy-done.18
  171.0 3.5 fusion.2
  174.5 8.1 %fusion.10 = f32[512,1536]{1,0:T(8,128)} fusion(bf16[512,2048]{1,0:T(8,128)(2,1)S(1)} %copy-done.15, bf16[1,1536,2048]{2,1,0:T(8,128)(2,1)} %get-tuple-element.58), kind=kOutput, calls=%fused_computation.14 | convolution fusion | flops 3221225472 | bytes 11534336 | tf_op jit(solution)/shard_map/dot_general | solution.py:1129
  182.6 8.5 %add_reduce_fusion = (f32[512]{0:T(512)S(1)}, bf16[512,1536]{1,0:T(8,128)(2,1)S(1)}, bf16[512,1536]{1,0:T(8,128)(2,1)}, bf16[512,1536]{1,0:T(8,128)(2,1)}) fusion(f32[512,1536]{1,0:T(8,128)S(1)} %fusion.2, f32[512,1536]{1,0:T(8,128)} %fusion.10, bf16[512,2048]{1,0:T(8,128)(2,1)S(1)} %multiply_convert_fusion, bf16[1,1536,2048]{2,1,0:T(8,128)(2,1)S(1)} %bitcast.163), kind=kOutput, calls=%fused_computation.39 | convolution fusion | flops 3238526464 | bytes 19400704 | tf_op jit(solution)/shard_map/dot_general | solution.py:1129
  191.1 8.1 %fusion.25.mlp_part = bf16[512,2048]{1,0:T(8,128)(2,1)} fusion(bf16[512,1536]{1,0:T(8,128)(2,1)} %get-tuple-element.156, bf16[1,1536,2048]{2,1,0:T(8,128)(2,1)} %get-tuple-element.58), kind=kOutput, calls=%fused_computation.44 | convolution fusion | flops 3222274048 | bytes 9961472 | tf_op jit(solution)/shard_map/dot_general | solution.py:1121
  199.2 3.5 fusion
  202.7 6.0 %subtract_convert_fusion = (bf16[512,2048]{1,0:T(8,128)(2,1)}, f32[512,2048]{1,0:T(8,128)}) fusion(bf16[512,2048]{1,0:T(8,128)(2,1)S(1)} %copy-done.1, bf16[512,2048]{1,0:T(8,128)(2,1)S(1)} %copy-done, f32[512]{0:T(512)S(1)} %multiply_multiply_fusion.1, f32[2048]{0:T(1024)S(1)} %bitcast.144, f32[512]{0:T(512)S(1)} %add_rsqrt_fusion, ...), kind=kOutput, calls=%fused_computation.26 | convolution fusion | flops 3230662656 | bytes 22556672 | tf_op jit(solution)/shard_map/dot_general | solution.py:1121
  208.7 5.4 %convolution_convert_fusion = bf16[1536,2048]{1,0:T(8,128)(2,1)} fusion(bf16[512,1536]{1,0:T(8,128)(2,1)S(1)} %get-tuple-element.153, bf16[512,2048]{1,0:T(8,128)(2,1)S(1)} %multiply_convert_fusion), kind=kOutput, calls=%fused_computation.1 | convolution fusion | flops 3224371200 | bytes 9961472 | tf_op jit(solution)/shard_map/dot_general | solution.py:1125
  214.2 5.4 %convolution_convert_fusion.1 = bf16[1536,2048]{1,0:T(8,128)(2,1)} fusion(bf16[512,1536]{1,0:T(8,128)(2,1)S(1)} %copy-done.24, bf16[512,2048]{1,0:T(8,128)(2,1)S(1)} %multiply_convert_fusion), kind=kOutput, calls=%fused_computation.2 | convolution fusion | flops 3224371200 | bytes 9961472 | tf_op jit(solution)/shard_map/dot_general | solution.py:1125
  219.6 5.6 %convolution_convert_fusion.2 = bf16[1536,2048]{1,0:T(8,128)(2,1)} fusion(bf16[512,1536]{1,0:T(8,128)(2,1)S(1)} %copy-done.23, bf16[512,2048]{1,0:T(8,128)(2,1)S(1)} %copy-done.15), kind=kOutput, calls=%fused_computation.3 | convolution fusion | flops 3224371200 | bytes 9961472 | tf_op jit(solution)/shard_map/dot_general | solution.py:1125
  225.1 59.8 %resid_sum.1 = (bf16[512,2048]{1,0:T(8,128)(2,1)}, f32[512,512]{1,0:T(8,128)}, f32[384,256]{1,0:T(8,128)}, f32[384,256]{1,0:T(8,128)}) custom-call(bf16[512,2048]{1,0:T(8,128)(2,1)} %get-tuple-element.188.part, bf16[4,384,2048]{2,1,0:T(8,128)(2,1)} %bitcast.122, bf16[4,384,2048]{2,1,0:T(8,128)(2,1)} %bitcast.121), custom_call_target="tpu_custom_call" | custom-call | tf_op jit(solution)/shard_map/resid_sum/pallas_call | solution.py:269
  285.0 3.1 convert_add_fusion.1
  288.0 0.9 copy.56
  288.9 5.9 %fusion.31.dhy = f32[512,640]{1,0:T(8,128)} fusion(bf16[3,640,2048]{2,1,0:T(8,128)(2,1)} %get-tuple-element.65, bf16[512,2048]{1,0:T(8,128)(2,1)} %get-tuple-element.64, bf16[512,2048]{1,0:T(8,128)(2,1)} %get-tuple-element.57), kind=kOutput, calls=%fused_computation.48 | convolution fusion | flops 1346371584 | bytes 8126464 | tf_op jit(solution)/shard_map/dot_general | solution.py:1129
  294.9 58.7 %backward_scan.1 = (bf16[512,640]{1,0:T(8,128)(2,1)}, bf16[512,640]{1,0:T(8,128)(2,1)}, f32[640,1280]{1,0:T(8,128)}, f32[8,640]{1,0:T(8,128)}, bf16[2048,128]{1,0:T(8,128)(2,1)}, /*index=5*/f32[384,256]{1,0:T(8,128)}) custom-call(f32[512,640]{1,0:T(8,128)} %fusion.31.dhy, f32[512,640]{1,0:T(8,128)} %get-tuple-element.66.yb, ...), custom_call_target="tpu_custom_call" | custom-call | tf_op jit(solution)/shard_map/backward_scan/pallas_call | solution.py:1084
  353.6 3.2 convolution_convert_fusion.3
  356.9 0.4 add_reduce_fusion.1
  357.3 0.3 copy-done.17
  357.6 0.1 fusion.41
  357.7 0.1 copy.55
  357.8 1.2 slice_reduce_fusion
  359.0 0.9 copy.57
  359.9 1.8 fusion.37
  361.8 0.2 maximum_bitcast_fusion
  362.0 1.3 pad_maximum_fusion.1.blocks
  363.2 0.9 copy-done.19
  364.1 1.6 convolution_convert_fusion.5
  365.7 1.6 convolution_convert_fusion.4
  367.3 0.1 copy-done.4
  367.4 4.0 pad_maximum_fusion.rec
  371.5 1.0 slice-done.1
  372.5 1.8 fusion.29
  374.3 1.0 copy-done.22
  375.3 4.5 fusion.15
  379.9 0.7 maximum_maximum_fusion.gains
  380.6 70.4 %last_sums.1 = (bf16[2048,128]{1,0:T(8,128)(2,1)}, f32[480,256]{1,0:T(8,128)}, f32[384,160]{1,0:T(8,128)}, f32[8,128]{1,0:T(8,128)}) custom-call(bf16[512,2048]{1,0:T(8,128)(2,1)} %get-tuple-element.155.part, f32[512,512]{1,0:T(8,128)} %get-tuple-element.190.dz, bf16[4,480,2048]{2,1,0:T(8,128)(2,1)} %pad_maximum_fusion.rec, ...), custom_call_target="tpu_custom_call" | custom-call | tf_op jit(solution)/shard_map/last_sums/pallas_call | solution.py:565
  451.0 1.3 slice_bitcast_fusion.4
  452.3 1.3 slice.141
  453.6 1.4 fusion.39
  455.0 1.7 slice_bitcast_fusion
  456.7 1.9 fusion.38
  458.6 2.1 convert_element_type.108
  460.7 0.8 copy.65
  461.5 0.7 copy.66
  (66 shorter events, 0.2 us)
Async XLA Ops:
  11.1 1.8 copy-start.11
  163.9 4.3 copy-start
  163.9 4.3 copy-start.1
  168.2 2.8 copy-start.18
  171.0 3.5 copy-start.15
  171.0 11.6 %slice-start.2 = ((s8[6291456]{0:T(1024)(128)(4,1)}), s8[4194304]{0:T(1024)(128)(4,1)S(1)}, s32[]{:S(2)}) async-start(s8[6291456]{0:T(1024)(128)(4,1)} %bitcast.162), calls=%async_computation.2 | async-start | bytes 8388608
  174.5 8.1 %slice-start.3 = ((s8[6291456]{0:T(1024)(128)(4,1)}), s8[2097152]{0:T(1024)(128)(4,1)S(1)}, s32[]{:S(2)}) async-start(s8[6291456]{0:T(1024)(128)(4,1)} %bitcast.162), calls=%async_computation.3 | async-start | bytes 4194304
  191.1 8.1 %copy-start.24 = (bf16[512,1536]{1,0:T(8,128)(2,1)S(1)}, bf16[512,1536]{1,0:T(8,128)(2,1)}, u32[]{:S(2)}) copy-start(bf16[512,1536]{1,0:T(8,128)(2,1)} %get-tuple-element.154) | copy-start | bytes 4718596
  214.2 5.4 %copy-start.23 = (bf16[512,1536]{1,0:T(8,128)(2,1)S(1)}, bf16[512,1536]{1,0:T(8,128)(2,1)}, u32[]{:S(2)}) copy-start(bf16[512,1536]{1,0:T(8,128)(2,1)} %get-tuple-element.156) | copy-start | bytes 4718596
  225.1 59.8 %copy-start.6 = (f32[512,512]{1,0:T(8,128)S(1)}, f32[512,512]{1,0:T(8,128)}, u32[]{:S(2)}) copy-start(f32[512,512]{1,0:T(8,128)} %get-tuple-element.79) | copy-start | bytes 3145732
  284.9 3.1 copy-start.14
  294.9 58.7 %copy-start.16 = (bf16[512,2048]{1,0:T(8,128)(2,1)S(1)}, bf16[512,2048]{1,0:T(8,128)(2,1)}, u32[]{:S(2)}) copy-start(bf16[512,2048]{1,0:T(8,128)(2,1)} %get-tuple-element.57) | copy-start | bytes 6291460
  294.9 58.7 %copy-start.20 = (bf16[512,2048]{1,0:T(8,128)(2,1)S(1)}, bf16[512,2048]{1,0:T(8,128)(2,1)}, u32[]{:S(2)}) copy-start(bf16[512,2048]{1,0:T(8,128)(2,1)} %get-tuple-element.64) | copy-start | bytes 6291460
  294.9 58.7 %copy-start.21 = (bf16[512,640]{1,0:T(8,128)(2,1)S(1)}, bf16[512,640]{1,0:T(8,128)(2,1)}, u32[]{:S(2)}) copy-start(bf16[512,640]{1,0:T(8,128)(2,1)} %get-tuple-element.87) | copy-start | bytes 1966084
  353.6 3.3 copy-start.3
  353.6 3.3 copy-start.5
  353.6 3.3 copy-start.7
  353.6 3.3 copy-start.8
  356.9 0.7 copy-start.17
  356.9 2.1 copy-start.13
  361.7 1.5 copy-start.9
  361.8 2.4 copy-start.19
  365.7 1.7 copy-start.4
  365.7 5.8 %slice-start = ((s8[7864320]{0:T(1024)(128)(4,1)}), s8[4194304]{0:T(1024)(128)(4,1)S(1)}, s32[]{:S(2)}) async-start(s8[7864320]{0:T(1024)(128)(4,1)} %bitcast.160), calls=%async_computation | async-start | bytes 8388608
  367.4 5.1 %slice-start.1 = ((s8[7864320]{0:T(1024)(128)(4,1)}), s8[3670016]{0:T(1024)(128)(4,1)S(1)}, s32[]{:S(2)}) async-start(s8[7864320]{0:T(1024)(128)(4,1)} %bitcast.160), calls=%async_computation.1 | async-start | bytes 7340032
  372.5 1.8 copy-start.2
  372.5 2.8 copy-start.22
  451.0 9.7 %copy-start.10 = (bf16[2048,128]{1,0:T(8,128)(2,1)S(1)}, bf16[2048,128]{1,0:T(8,128)(2,1)}, u32[]{:S(2)}) copy-start(bf16[2048,128]{1,0:T(8,128)(2,1)} %get-tuple-element.209) | copy-start | bytes 1572868
  451.0 10.5 %copy-start.12 = (f32[384,256]{1,0:T(8,128)S(1)}, f32[384,256]{1,0:T(8,128)}, u32[]{:S(2)}) copy-start(f32[384,256]{1,0:T(8,128)} %get-tuple-element.225) | copy-start | bytes 1179652
